TPU v7x, 512 devices: a whole 4x8x8 slice. The times are simulated.
512 devices in a mesh: seq: 8 (over y), exp: 16 (over z, core), tp: 4 (over x).
Axes of the slice: x: 4, y: 8, z: 8, core: 2. Of those that a mesh axis runs over, the one named last changes fastest.
Arguments:
- tokens: bfloat16 [4096, 4096], P(('seq', 'exp'), 'tp'), may hold values from -6 to 6
- expert_ids: int32 [4096, 8], P(('seq', 'exp')), may hold values from 0 to 15, all different within a row; in each aligned block of 32 rows (0 to 31, 32 to 63, ...) at most 24 rows name the same one
- route_weights: float32 [4096, 8], P(('seq', 'exp')), may hold values from 0.05 to 1
- expert_gate: bfloat16 [16, 4096, 512], P('exp', None, 'tp'), may hold values from -0.09375 to 0.09375
- expert_up: bfloat16 [16, 4096, 512], P('exp', None, 'tp'), may hold values from -0.09375 to 0.09375
- expert_down: bfloat16 [16, 512, 4096], P('exp', None, 'tp'), may hold values from -0.25 to 0.25
- student_gate: bfloat16 [4096, 8192], P('seq', ('exp', 'tp')), may hold values from -0.09375 to 0.09375
- student_up: bfloat16 [4096, 8192], P('seq', ('exp', 'tp')), may hold values from -0.09375 to 0.09375
- student_down: bfloat16 [8192, 4096], P(('exp', 'tp'), 'seq'), may hold values from -0.0625 to 0.0625
- out_grad: bfloat16 [4096, 4096], P(('seq', 'exp'), 'tp'), may hold values from -6 to 6
Outputs:
- teacher_out: bfloat16 [4096, 4096], P(('seq', 'exp'), 'tp')
- grad_gate: float32 [4096, 8192], P('seq', ('exp', 'tp'))
- grad_up: float32 [4096, 8192], P('seq', ('exp', 'tp'))
- grad_down: float32 [8192, 4096], P(('exp', 'tp'), 'seq')
Inputs may be any that keep to these rules, and one draw needn't show every extreme that they name: `expert_ids`: the 8 ids of a row are distinct. Among the 32 rows of one device no id appears more than 24 times, and in every draw some device's rows name some id exactly 24 times.
All inputs are finite; a program needn't handle non-finite values.
Results may differ from a plain program's by a relative error of at most 0.019.
Values may be sent and summed in bfloat16 or wider, within the bound.
A program may use at most 64 MiB of HBM per device.

v0:
```python
import jax
import jax.numpy as jnp
from jax import lax
from jax.sharding import PartitionSpec as P

CAP = 24


def silu_grad(gate_sum):
    sigmoid_val = jax.nn.sigmoid(gate_sum)
    return sigmoid_val * (1.0 + gate_sum * (1.0 - sigmoid_val))


def body(
    tokens,
    expert_ids,
    route_weights,
    expert_gate,
    expert_up,
    expert_down,
    student_gate,
    student_up,
    student_down,
    out_grad,
):
    exp_count = lax.axis_size("exp")
    local_experts = expert_gate.shape[0]
    all_experts = exp_count * local_experts
    slot_count = CAP
    labels = jnp.arange(all_experts, dtype=jnp.int32)
    chosen = expert_ids[:, :, None] == labels[None, None, :]
    member = jnp.sum(chosen.astype(jnp.int32), axis=1)
    earlier = jnp.cumsum(member, axis=0) - member
    positions = jnp.arange(slot_count, dtype=jnp.int32)
    placed = (earlier[:, :, None] == positions[None, None, :]) & (member[:, :, None] == 1)
    weight_rows = jnp.sum(jnp.where(chosen, route_weights[:, :, None], 0.0), axis=1)
    combine_map = jnp.where(placed, weight_rows[:, :, None], 0.0)
    outgoing = jnp.einsum(
        "rec,rd->ecd", placed.astype(jnp.bfloat16), tokens, preferred_element_type=jnp.float32
    ).astype(jnp.bfloat16)
    outgoing = outgoing.reshape(exp_count, local_experts, slot_count, tokens.shape[1])
    portion = lax.all_gather(
        lax.all_to_all(outgoing, "exp", split_axis=0, concat_axis=0, tiled=True),
        "tp",
        axis=3,
        tiled=True,
    )
    gate_part = jnp.einsum(
        "sxcd,xdf->sxcf", portion, expert_gate, preferred_element_type=jnp.float32
    )
    up_part = jnp.einsum("sxcd,xdf->sxcf", portion, expert_up, preferred_element_type=jnp.float32)
    gate_sum = gate_part
    up_sum = up_part
    hidden = (jax.nn.silu(gate_sum) * up_sum).astype(jnp.bfloat16)
    expert_out = jnp.einsum(
        "sxcf,xfd->sxcd",
        lax.all_gather(hidden, "tp", axis=3, tiled=True),
        expert_down,
        preferred_element_type=jnp.float32,
    )
    returned = lax.all_to_all(
        expert_out.astype(jnp.bfloat16), "exp", split_axis=0, concat_axis=0, tiled=True
    )
    returned = returned.reshape(all_experts, slot_count, returned.shape[3]).astype(jnp.float32)
    teacher_out = jnp.einsum(
        "rec,ecd->rd", combine_map, returned, precision=lax.Precision.HIGHEST
    ).astype(jnp.bfloat16)
    wide_act, wide_grad = (
        lax.all_gather(teacher_out, "tp", axis=1, tiled=True),
        lax.all_gather(out_grad, "tp", axis=1, tiled=True),
    )
    act_rows, grad_rows = (
        lax.all_gather(wide_act, "exp", axis=0, tiled=True),
        lax.all_gather(wide_grad, "exp", axis=0, tiled=True),
    )
    columns = act_rows
    gate_part = jnp.dot(
        columns,
        lax.all_gather(student_gate, "seq", axis=0, tiled=True),
        preferred_element_type=jnp.float32,
    )
    up_part = jnp.dot(
        columns,
        lax.all_gather(student_up, "seq", axis=0, tiled=True),
        preferred_element_type=jnp.float32,
    )
    columns = grad_rows
    hidden_grad = lax.dot_general(
        columns,
        lax.all_gather(student_down, "seq", axis=1, tiled=True),
        (((1,), (1,)), ((), ())),
        preferred_element_type=jnp.float32,
    )
    activated = jax.nn.silu(gate_part)
    hidden = (activated * up_part).astype(jnp.bfloat16)
    gate_grad = (hidden_grad * up_part * silu_grad(gate_part)).astype(jnp.bfloat16)
    up_grad = (hidden_grad * activated).astype(jnp.bfloat16)
    contract_rows = (((0,), (0,)), ((), ()))
    down_term = lax.dot_general(
        hidden, grad_rows, contract_rows, preferred_element_type=jnp.float32
    )
    gate_term = lax.dot_general(
        act_rows, gate_grad, contract_rows, preferred_element_type=jnp.float32
    )
    up_term = lax.dot_general(act_rows, up_grad, contract_rows, preferred_element_type=jnp.float32)
    grad_gate, grad_up = (
        lax.psum_scatter(
            gate_term.astype(jnp.bfloat16), "seq", scatter_dimension=0, tiled=True
        ).astype(jnp.float32),
        lax.psum_scatter(
            up_term.astype(jnp.bfloat16), "seq", scatter_dimension=0, tiled=True
        ).astype(jnp.float32),
    )
    grad_down = lax.psum_scatter(
        down_term.astype(jnp.bfloat16), "seq", scatter_dimension=1, tiled=True
    ).astype(jnp.float32)
    return (teacher_out, grad_gate, grad_up, grad_down)


def solution(mesh):
    in_specs = (
        P(("seq", "exp"), "tp"),
        P(("seq", "exp"), None),
        P(("seq", "exp"), None),
        P("exp", None, "tp"),
        P("exp", None, "tp"),
        P("exp", None, "tp"),
        P("seq", ("exp", "tp")),
        P("seq", ("exp", "tp")),
        P(("exp", "tp"), "seq"),
        P(("seq", "exp"), "tp"),
    )
    out_specs = (
        P(("seq", "exp"), "tp"),
        P("seq", ("exp", "tp")),
        P("seq", ("exp", "tp")),
        P(("exp", "tp"), "seq"),
    )
    return jax.shard_map(body, mesh=mesh, in_specs=in_specs, out_specs=out_specs, check_vma=False)
```

profile of v0, /device:TPU:1, one launch (start us, length us, event | category | flops | bytes accessed | tf_op | source)
XLA Modules:
  0.0 440.6 jit_solution(741316703449857640)
XLA Ops:
  7.2 0.0 all-gather.7.cloned.1.call-start
  7.2 0.8 convert_reduce_fusion
  8.1 0.1 copy.25
  8.2 0.1 reduce_window_sum.11
  8.2 0.1 copy.27
  8.3 1.3 fusion.5
  9.6 34.7 %all_to_all.10 = bf16[16,1,24,1024]{3,2,1,0:T(8,128)(2,1)} all-to-all(bf16[16,1,24,1024]{3,2,1,0:T(8,128)(2,1)S(1)} %fusion.5), channel_id=1, replica_groups=mesh['seq'=8,'exp'=16,'tp'=4] {'exp'}, dimensions={0} | all-to-all | bytes 1572864 | tf_op jit(solution)/shard_map/all_to_all | solution.py:43
  44.3 0.0 all-gather.7.cloned.1.call-update
  44.3 0.0 all-gather.13.cloned.1.call-start
  44.3 0.7 all-gather.13.cloned.1.call-update
  45.0 0.0 all-gather.11.cloned.1.call-start
  45.1 12.4 %all_gather.31 = bf16[32,4096]{1,0:T(8,128)(2,1)} all-gather(bf16[32,1024]{1,0:T(8,128)(2,1)} %param.19), channel_id=1, replica_groups=mesh['seq'=8,'exp'=16,'tp'=4] {'tp'}, dimensions={1}, use_global_device_ids=true | all-gather | bytes 327680 | tf_op jit(solution)/shard_map/all_gather | solution.py:70
  57.5 0.0 all-gather.11.cloned.1.call-update
  57.5 0.0 all-gather.17.cloned.1.call-start
  57.5 0.5 all-gather.17.cloned.1.call-update
  58.1 27.8 %all-gather.7.cloned.1.call-done = bf16[16,1,24,4096]{3,2,0,1:T(8,128)(2,1)} async-done(((bf16[16,1,24,1024]{3,2,0,1:T(8,128)(2,1)}), bf16[16,1,24,4096]{3,2,0,1:T(8,128)(2,1)}) %all-gather.7.cloned.1.call-update) | async-done | bytes 3145744 | tf_op jit(solution)/shard_map/all_gather | solution.py:42
  85.8 3.0 fusion.6
  88.9 1.0 fusion.15
  89.9 9.5 %all_gather.28 = bf16[16,1,24,512]{3,2,0,1:T(8,128)(2,1)S(1)} all-gather(bf16[16,1,24,128]{3,2,0,1:T(8,128)(2,1)S(1)} %fusion.15), channel_id=1, replica_groups=mesh['seq'=8,'exp'=16,'tp'=4] {'tp'}, dimensions={3}, use_global_device_ids=true | all-gather | bytes 491520 | tf_op jit(solution)/shard_map/all_gather | solution.py:57
  99.5 1.5 fusion.4
  101.0 11.0 %all-to-all-start.1 = ((bf16[16,1,24,1024]{3,2,1,0:T(8,128)(2,1)}), bf16[16,1,24,1024]{3,2,1,0:T(8,128)(2,1)S(1)}, u32[]{:S(2)}, u32[]{:S(2)}) async-start(bf16[16,1,24,1024]{3,2,1,0:T(8,128)(2,1)} %fusion.4), calls=%async_computation.1 | async-start | bytes 1572864 | tf_op jit(solution)/shard_map/all_to_all | solution.py:61
  112.0 0.0 all-gather.9.cloned.1.call-start
  112.1 22.6 %all-to-all-done.1 = bf16[16,1,24,1024]{3,2,1,0:T(8,128)(2,1)S(1)} async-done(((bf16[16,1,24,1024]{3,2,1,0:T(8,128)(2,1)}), bf16[16,1,24,1024]{3,2,1,0:T(8,128)(2,1)S(1)}, u32[]{:S(2)}, u32[]{:S(2)}) %all-to-all-start.1) | async-done | bytes 786464 | tf_op jit(solution)/shard_map/all_to_all | solution.py:61
  134.7 0.5 fusion.18
  135.2 10.5 %all_gather.29 = bf16[32,4096]{1,0:T(8,128)(2,1)} all-gather(bf16[32,1024]{1,0:T(8,128)(2,1)S(1)} %fusion.18), channel_id=1, replica_groups=mesh['seq'=8,'exp'=16,'tp'=4] {'tp'}, dimensions={1}, use_global_device_ids=true | all-gather | bytes 327680 | tf_op jit(solution)/shard_map/all_gather | solution.py:69
  145.7 0.0 all-gather.9.cloned.1.call-update
  145.7 0.0 all-gather.15.cloned.1.call-start
  145.7 0.5 all-gather.15.cloned.1.call-update
  146.3 0.0 reduce-scatter.4.cloned.1.call-start
  146.3 0.0 all-gather.13.cloned.1.call-done
  146.3 30.0 %all-gather.11.cloned.1.call-done = bf16[512,4096]{1,0:T(8,128)(2,1)} async-done(((bf16[32,4096]{1,0:T(8,128)(2,1)}), bf16[512,4096]{1,0:T(8,128)(2,1)}) %all-gather.11.cloned.1.call-update) | async-done | bytes 4194320 | tf_op jit(solution)/shard_map/all_gather | solution.py:74
  176.3 3.7 fusion.43
  180.1 32.0 %all-gather.17.cloned.1.call-done = bf16[4096,128]{1,0:T(8,128)(2,1)} async-done(((bf16[512,128]{1,0:T(8,128)(2,1)}), bf16[4096,128]{1,0:T(8,128)(2,1)}) %all-gather.17.cloned.1.call-update) | async-done | bytes 1048592 | tf_op jit(solution)/shard_map/all_gather | solution.py:79
  212.1 51.7 %all-gather.9.cloned.1.call-done = bf16[512,4096]{1,0:T(8,128)(2,1)} async-done(((bf16[32,4096]{1,0:T(8,128)(2,1)}), bf16[512,4096]{1,0:T(8,128)(2,1)}) %all-gather.9.cloned.1.call-update) | async-done | bytes 4194320 | tf_op jit(solution)/shard_map/all_gather | solution.py:73
  263.8 3.7 fusion.45
  267.6 32.0 %all-gather.15.cloned.1.call-done = bf16[4096,128]{1,0:T(8,128)(2,1)} async-done(((bf16[512,128]{1,0:T(8,128)(2,1)}), bf16[4096,128]{1,0:T(8,128)(2,1)}) %all-gather.15.cloned.1.call-update) | async-done | bytes 1048592 | tf_op jit(solution)/shard_map/all_gather | solution.py:84
  299.6 3.9 fusion.44
  303.5 2.4 convolution_convert_fusion.2
  306.0 0.0 reduce-scatter.8.cloned.1.call-start
  306.0 4.0 convolution_convert_fusion
  310.0 0.0 reduce-scatter.6.cloned.1.call-start
  310.0 4.5 %convolution_convert_fusion.1 = bf16[4096,128]{1,0:T(8,128)(2,1)} fusion(bf16[512,4096]{1,0:T(8,128)(2,1)} %all-gather.9.cloned.1.call-done, f32[512,128]{1,0:T(8,128)S(1)} %fusion.43, f32[512,128]{1,0:T(8,128)S(1)} %fusion.45), kind=kOutput, calls=%fused_computation.1 | convolution fusion | flops 537788416 | bytes 5767168 | tf_op jit(solution)/shard_map/dot_general | solution.py:105
  314.6 31.8 %reduce-scatter.4.cloned.1.call-done = bf16[512,128]{1,0:T(8,128)(2,1)} async-done(((bf16[4096,128]{1,0:T(8,128)(2,1)}), bf16[512,128]{1,0:T(8,128)(2,1)}) %reduce-scatter.4.cloned.1.call-update) | async-done | bytes 131088 | tf_op jit(solution)/shard_map/reduce_scatter | solution.py:107
  346.4 1.6 convert_element_type.63
  348.0 41.4 %reduce-scatter.8.cloned.1.call-done = bf16[128,512]{1,0:T(8,128)(2,1)} async-done(((bf16[128,4096]{1,0:T(8,128)(2,1)}), bf16[128,512]{1,0:T(8,128)(2,1)}) %reduce-scatter.8.cloned.1.call-update) | async-done | bytes 131088 | tf_op jit(solution)/shard_map/reduce_scatter | solution.py:114
  389.4 1.6 convert_element_type.69
  391.1 41.4 %reduce-scatter.6.cloned.1.call-done = bf16[512,128]{1,0:T(8,128)(2,1)} async-done(((bf16[4096,128]{1,0:T(8,128)(2,1)}), bf16[512,128]{1,0:T(8,128)(2,1)}) %reduce-scatter.6.cloned.1.call-update) | async-done | bytes 131088 | tf_op jit(solution)/shard_map/reduce_scatter | solution.py:110
  432.5 1.6 convert_element_type.66
  (22 shorter events, 0.1 us)
Async XLA Ops:
  7.2 92.3 %copy-start = (bf16[1,512,1024]{2,1,0:T(8,128)(2,1)S(1)}, bf16[1,512,1024]{2,1,0:T(8,128)(2,1)}, u32[]{:S(2)}) copy-start(bf16[1,512,1024]{2,1,0:T(8,128)(2,1)} %param.15) | copy-start | bytes 3145732
  7.2 78.6 %copy-start.3 = (bf16[1,4096,128]{2,1,0:T(8,128)(2,1)S(1)}, bf16[1,4096,128]{2,1,0:T(8,128)(2,1)}, u32[]{:S(2)}) copy-start(bf16[1,4096,128]{2,1,0:T(8,128)(2,1)} %param.13) | copy-start | bytes 3145732
  7.2 78.6 %all-gather.7.cloned.1.call-start = ((), (), s32[]{:S(2)}) async-start(), calls=%async_computation.5 | async-start | bytes 3932160 | tf_op jit(solution)/shard_map/all_gather | solution.py:42
  8.3 80.6 %copy-start.7 = (bf16[1,4096,128]{2,1,0:T(8,128)(2,1)S(1)}, bf16[1,4096,128]{2,1,0:T(8,128)(2,1)}, u32[]{:S(2)}) copy-start(bf16[1,4096,128]{2,1,0:T(8,128)(2,1)} %param.14) | copy-start | bytes 3145732
  44.3 102.1 %all-gather.13.cloned.1.call-start = ((), (), s32[]{:S(2)}) async-start(), calls=%async_computation.8 | async-start | bytes 1179648 | tf_op jit(solution)/shard_map/all_gather | solution.py:90
  45.0 131.3 %all-gather.11.cloned.1.call-start = ((), (), s32[]{:S(2)}) async-start(), calls=%async_computation.7 | async-start | bytes 4456448 | tf_op jit(solution)/shard_map/all_gather | solution.py:74
  57.5 154.6 %all-gather.17.cloned.1.call-start = ((), (), s32[]{:S(2)}) async-start(), calls=%async_computation.10 | async-start | bytes 1179648 | tf_op jit(solution)/shard_map/all_gather | solution.py:79
  85.8 3.0 copy-start.2
  88.9 23.2 %copy-start.5 = (s32[32,8]{0,1:T(8,128)S(1)}, s32[32,8]{0,1:T(8,128)}, u32[]{:S(2)}) copy-start(s32[32,8]{0,1:T(8,128)} %param.11) | copy-start | bytes 3076
  88.9 23.2 %copy-start.6 = (f32[32,8]{0,1:T(8,128)S(1)}, f32[32,8]{0,1:T(8,128)}, u32[]{:S(2)}) copy-start(f32[32,8]{0,1:T(8,128)} %param.12) | copy-start | bytes 3076
  101.0 33.7 %all-to-all-start.1 = ((bf16[16,1,24,1024]{3,2,1,0:T(8,128)(2,1)}), bf16[16,1,24,1024]{3,2,1,0:T(8,128)(2,1)S(1)}, u32[]{:S(2)}, u32[]{:S(2)}) async-start(bf16[16,1,24,1024]{3,2,1,0:T(8,128)(2,1)} %fusion.4), calls=%async_computation.1 | async-start | bytes 1572864 | tf_op jit(solution)/shard_map/all_to_all | solution.py:61
  112.0 151.8 %all-gather.9.cloned.1.call-start = ((), (), s32[]{:S(2)}) async-start(), calls=%async_computation.6 | async-start | bytes 4456448 | tf_op jit(solution)/shard_map/all_gather | solution.py:73
  135.2 132.4 %copy-start.4 = (bf16[32,1024]{1,0:T(8,128)(2,1)}, bf16[32,1024]{1,0:T(8,128)(2,1)S(1)}, u32[]{:S(2)}) copy-start(bf16[32,1024]{1,0:T(8,128)(2,1)S(1)} %fusion.18) | copy-start | bytes 196612
  145.7 153.9 %all-gather.15.cloned.1.call-start = ((), (), s32[]{:S(2)}) async-start(), calls=%async_computation.9 | async-start | bytes 1179648 | tf_op jit(solution)/shard_map/all_gather | solution.py:84
  146.3 200.1 %reduce-scatter.4.cloned.1.call-start = ((), (), s32[]{:S(2)}) async-start(), calls=%async_computation.11 | async-start | bytes 1179648 | tf_op jit(solution)/shard_map/reduce_scatter | solution.py:107
  299.6 3.9 copy-start.1
  306.0 83.5 %reduce-scatter.8.cloned.1.call-start = ((), (), s32[]{:S(2)}) async-start(), calls=%async_computation.13 | async-start | bytes 1179648 | tf_op jit(solution)/shard_map/reduce_scatter | solution.py:114
  310.0 122.5 %reduce-scatter.6.cloned.1.call-start = ((), (), s32[]{:S(2)}) async-start(), calls=%async_computation.12 | async-start | bytes 1179648 | tf_op jit(solution)/shard_map/reduce_scatter | solution.py:110
Sparse Core Ops, SparseCore 0:
  44.4 41.3 all-gather.6
  87.9 37.2 all-gather.12
  127.3 48.9 all-gather.10
  178.2 33.7 all-gather.16
  214.0 49.7 all-gather.8
  265.8 33.7 all-gather.14
  306.1 40.2 reduce-scatter.3
  349.2 40.1 reduce-scatter.7
  392.3 40.1 reduce-scatter.5
where the time goes:
time: 445 us; the launch traced here: 441 us
  waiting for transfers between devices  313 us (70%)
  blocking collectives  67.1 us (15%)
  matrix products  29.6 us (7%)
  between operations  14 us (3%)
  starting transfers between devices  11.4 us (3%)
  other arithmetic  5.8 us (1%)
    all_gather x1, waiting for transfers between devices, body(): lax.all_gather(wide_act, 'exp', axis=0, tiled=True)  51.7 us
    reduce_scatter x1, waiting for transfers between devices, body(): lax.psum_scatter(down_term.astype(jnp.bfloat16), 'seq', scatter_dimension...  41.4 us
    reduce_scatter x1, waiting for transfers between devices, body(): lax.psum_scatter(up_term.astype(jnp.bfloat16), 'seq', scatter_dimension=0...  41.4 us
    all_to_all x1, blocking collectives, body(): lax.all_to_all(outgoing, 'exp', split_axis=0, concat_axis=0, tiled=True)  34.7 us
    all_gather x1, waiting for transfers between devices, body(): lax.all_gather(student_gate, 'seq', axis=0, tiled=True)  32 us
    all_gather x1, waiting for transfers between devices, body(): lax.all_gather(student_up, 'seq', axis=0, tiled=True)  32 us
    reduce_scatter x1, waiting for transfers between devices, body(): lax.psum_scatter(gate_term.astype(jnp.bfloat16), 'seq', scatter_dimension...  31.8 us
    all_gather x1, waiting for transfers between devices, body(): lax.all_gather(wide_grad, 'exp', axis=0, tiled=True)  30 us
  transfers between devices with their start and end apart: 10, of which 9 were waited for; matrix products, arithmetic and copies ran while one was open for 6% of the time, Pallas kernels for 0%

commit v1 on v0

v1 whole, which is shorter than its diff:
```python
import jax
import jax.numpy as jnp
from jax import lax
from jax.experimental import pallas as pl
from jax.experimental.pallas import tpu as pltpu
from jax.sharding import PartitionSpec as P

MESH = pl.DeviceIdType.MESH
F32 = jnp.float32
BF16 = jnp.bfloat16
Z_ORDER = (0, 1, 7, 2, 6, 3, 5, 4)
Z_POS = {z: i for i, z in enumerate(Z_ORDER)}
N_RECV = 224
N_SEND = 64


def row_of(half, z, other=0):
    return other * 256 + half * 128 + Z_POS[z % 8] * 16


def sigmoid(a):
    return 1.0 / (1.0 + jnp.exp(-a))


class Agenda:
    def __init__(self):
        self.steps = []

    def at(self, time, step):
        self.steps.append((time, len(self.steps), step))

    def run(self):
        for _, _, step in sorted(self.steps, key=lambda s: (s[0], s[1])):
            step()


def kernel(
    tokens, ids, weights, egate, eup, edown, sgate, sup, sdown, ograd,
    t_out, gg_out, gu_out, gd_out,
    tok, act, dout, wt, wed, wgu, wd, hid, coef, part, sibp, rsb, gu, hg, gt, grad, ring,
    send_sems, recv_sems, local_sems,
):
    yo = lax.axis_index("seq")
    eo = lax.axis_index("exp")
    xo = lax.axis_index("tp")
    zo = eo // 2
    co = lax.rem(eo, 2)

    def z_dev(d):
        return (yo, lax.rem(zo + d + 8, 8) * 2 + co, xo)

    def x_dev(d):
        return (yo, eo, lax.rem(xo + d + 4, 4))

    def y_dev(d):
        return (lax.rem(yo + d + 8, 8), eo, xo)

    sib = (yo, zo * 2 + (1 - co), xo)
    agenda = Agenda()
    drains = []
    counts = {"send": 0, "recv": 0, "local": 0}

    def new_send():
        counts["send"] += 1
        assert counts["send"] <= N_SEND
        return send_sems.at[counts["send"] - 1]

    def new_recv():
        counts["recv"] += 1
        assert counts["recv"] <= N_RECV
        return recv_sems.at[counts["recv"] - 1]

    def send(src, dst, s_sem, r_sem, device):
        pltpu.make_async_remote_copy(
            src_ref=src, dst_ref=dst, send_sem=s_sem, recv_sem=r_sem,
            device_id=device, device_id_type=MESH,
        ).start()

    def wait_recv(ref, r_sem):
        pltpu.make_async_remote_copy(
            src_ref=ref, dst_ref=ref, send_sem=send_sems.at[0], recv_sem=r_sem,
            device_id=sib, device_id_type=MESH,
        ).wait_recv()

    def drain(ref, s_sem):
        def step():
            pltpu.make_async_remote_copy(
                src_ref=ref, dst_ref=ref, send_sem=s_sem, recv_sem=recv_sems.at[0],
                device_id=sib, device_id_type=MESH,
            ).wait_send()

        drains.append(step)

    local = []

    def load(src, dst):
        copy = pltpu.make_async_copy(src, dst, local_sems.at[len(local)])
        copy.start()
        local.append(copy)
        return copy

    first = [
        load(tokens.at[pl.ds(0, 16)], tok.at[0, pl.ds(0, 16)]),
        load(tokens.at[pl.ds(16, 16)], tok.at[0, pl.ds(128, 16)]),
        load(sgate, wgu.at[pl.ds(pl.multiple_of(yo * 512, 512), 512), pl.ds(0, 128)]),
        load(sup, wgu.at[pl.ds(pl.multiple_of(yo * 512, 512), 512), pl.ds(128, 128)]),
        load(sdown, wd.at[yo]),
        load(ograd.at[pl.ds(0, 16)], dout.at[0, pl.ds(0, 16)]),
        load(ograd.at[pl.ds(16, 16)], dout.at[0, pl.ds(128, 16)]),
    ]
    later = [
        load(egate.at[0], wt.at[:, pl.ds(0, 128)]),
        load(eup.at[0], wt.at[:, pl.ds(128, 128)]),
        load(edown.at[0], wed),
    ]

    barrier = pltpu.get_barrier_semaphore()
    peers = [z_dev(d) for d in range(1, 8)] + [x_dev(d) for d in range(1, 4)] + [y_dev(1), y_dev(-1), sib]
    for device in peers:
        pl.semaphore_signal(barrier, inc=1, device_id=device, device_id_type=MESH)

    lane = lax.broadcasted_iota(jnp.int32, (16, 128), 1)
    lane_e = lax.rem(lane, 16)
    lane_half = lax.rem(lane // 16, 2)
    halves = []
    for half in range(2):
        total = jnp.zeros((16, 128), F32)
        for k in range(8):
            name = ids[half * 16 : half * 16 + 16, k : k + 1]
            weight = weights[half * 16 : half * 16 + 16, k : k + 1]
            total = total + jnp.where(lane_e == name, weight, 0.0)
        halves.append(total)
    value = jnp.where(lane_half == 0, halves[0], halves[1])
    high = value.astype(BF16).astype(F32)
    value = jnp.where(lane < 32, high, jnp.where(lane < 64, value - high, 0.0))
    coef[0, 0] = value.astype(BF16)

    pl.semaphore_wait(barrier, len(peers))
    for copy in first:
        copy.wait()

    def gather(buf, t0):
        s_z0, s_x0, s_b0 = new_send(), [new_send() for _ in range(3)], new_send()
        s_x1, s_z1, s_b1 = new_send(), new_send(), new_send()
        r_z0 = {(d, k): new_recv() for d in "RL" for k in range(1, 5)}
        r_x0 = {rel: new_recv() for rel in (1, 2, 3)}
        r_x1 = {rel: new_recv() for rel in (1, 2, 3)}
        r_z1 = {(d, k, c): new_recv() for d in "RL" for k in range(1, 5) for c in "ab"}
        r_b0, r_b1 = new_recv(), new_recv()
        step_dev = {"R": z_dev(1), "L": z_dev(-1)}

        def came(d, k):
            return (8 - k) % 8 if d == "R" else k % 8

        def z0_ref(d, k):
            rows = pl.ds(row_of(0, came(d, k)), 16)
            if k == 4:
                return buf.at[0, rows, pl.ds(0 if d == "R" else 512, 512)]
            return buf.at[0, rows]

        def z0_send(d, k):
            src = buf.at[0, pl.ds(row_of(0, came(d, k - 1)), 16)]
            if k == 4:
                src = buf.at[0, pl.ds(row_of(0, came(d, 3)), 16), pl.ds(0 if d == "R" else 512, 512)]
            send(src, z0_ref(d, k), s_z0, r_z0[d, k], step_dev[d])

        def x0_piece(r0, n):
            for i, d in enumerate((1, -1, 2)):
                send(
                    buf.at[0, pl.ds(r0, n)], buf.at[(-d) % 4, pl.ds(r0, n)], s_x0[i], r_x0[(-d) % 4], x_dev(d)
                )

        def z1_ref(z, c):
            rows = pl.ds(row_of(1, z), 16)
            return buf.at[pl.ds(0 if c == "a" else 2, 2), rows]

        def z1_send(d, k, c):
            send(z1_ref(came(d, k - 1), c), z1_ref(came(d, k), c), s_z1, r_z1[d, k, c], step_dev[d])

        def b0_send(rel):
            send(buf.at[rel, pl.ds(0, 128)], buf.at[rel, pl.ds(256, 128)], s_b0, r_b0, sib)

        def b1_send(z):
            send(
                buf.at[:, pl.ds(row_of(1, z), 16)], buf.at[:, pl.ds(row_of(1, z, 1), 16)], s_b1, r_b1, sib
            )

        def begin():
            own = pl.ds(128, 16)
            for d in (1, -1, 2):
                send(buf.at[0, own], buf.at[(-d) % 4, own], s_x1, r_x1[(-d) % 4], x_dev(d))
            for d in "RL":
                z0_send(d, 1)

        agenda.at(t0, begin)

        def z0_hop(k):
            for d in "RL":
                wait_recv(z0_ref(d, k), r_z0[d, k])
                if k < 4:
                    z0_send(d, k + 1)
            if k == 1:
                x0_piece(0, 48)
            if k == 2:
                x0_piece(48, 32)
            if k == 4:
                x0_piece(80, 48)
                b0_send(0)

        for k in range(1, 5):
            agenda.at(t0 + 2.7 * k, lambda k=k: z0_hop(k))

        def x0_done(rel):
            wait_recv(buf.at[rel, pl.ds(0, 128)], r_x0[rel])
            b0_send(rel)

        for i, rel in enumerate((1, 3, 2)):
            agenda.at(t0 + 15.5 + 0.4 * i, lambda rel=rel: x0_done(rel))

        def x1_done():
            own = pl.ds(128, 16)
            wait_recv(buf.at[1, own], r_x1[1])
            for d in "RL":
                z1_send(d, 1, "a")
            for rel in (2, 3):
                wait_recv(buf.at[rel, own], r_x1[rel])
            for d in "RL":
                z1_send(d, 1, "b")
            b1_send(0)

        agenda.at(t0 + 3.0, x1_done)

        def z1_hop(k, c):
            for d in "RL":
                if k == 4 and (d == "R") != (c == "a"):
                    continue
                z = came(d, k)
                wait_recv(z1_ref(z, c), r_z1[d, k, c])
                if k < 3 or (k == 3 and (d == "R") == (c == "a")):
                    z1_send(d, k + 1, c)
                if c == "b":
                    b1_send(z)

        for k in range(1, 5):
            agenda.at(t0 + 3.0 + 3.45 * k, lambda k=k: z1_hop(k, "a"))
            agenda.at(t0 + 4.4 + 3.45 * k, lambda k=k: z1_hop(k, "b"))

        def finish():
            wait_recv(buf.at[:, pl.ds(256, 128)], r_b0)
            wait_recv(buf.at[:, pl.ds(384, 128)], r_b1)

        done = t0 + 19.6
        agenda.at(done, finish)
        drain(buf.at[0, pl.ds(16, 112)], s_z0)
        for sem in s_x0:
            drain(buf.at[0, pl.ds(0, 128)], sem)
        drain(buf.at[:, pl.ds(0, 128)], s_b0)
        drain(buf.at[pl.ds(1, 3), pl.ds(128, 16)], s_x1)
        drain(buf.at[:, pl.ds(144, 112)], s_z1)
        drain(buf.at[:, pl.ds(128, 128)], s_b1)
        return done

    s_yw = [new_send() for _ in range(3)]
    r_yw = {(d, k, a): new_recv() for d in "RL" for k in range(1, 5) for a in range(3)}

    def yw_ref(a, origin, d, k):
        if a < 2:
            start, n = origin * 512, 512
            if k == 4:
                start, n = start + (0 if d == "R" else 256), 256
            return wgu.at[pl.ds(pl.multiple_of(start, 256), n), pl.ds(a * 128, 128)]
        if k == 4:
            return wd.at[origin, pl.ds(0 if d == "R" else 64, 64)]
        return wd.at[origin]

    def yw_origin(d, k):
        return lax.rem(yo + (8 - k if d == "R" else k), 8)

    def yw_send(d, k, a):
        ref = yw_ref(a, yw_origin(d, k - 1), d, k)
        send(ref, ref, s_yw[a], r_yw[d, k, a], y_dev(1 if d == "R" else -1))

    def yw_start():
        for a in range(3):
            for d in "RL":
                yw_send(d, 1, a)

    def yw_hop(k, a):
        for d in "RL":
            wait_recv(yw_ref(a, yw_origin(d, k), d, k), r_yw[d, k, a])
            if k < 4:
                yw_send(d, k + 1, a)

    agenda.at(0.0, yw_start)
    for k in range(1, 5):
        for a in range(3):
            when = 8.9 * (k - 1) + 2.95 * (a + 1) + 2.0 if k < 4 else 8.9 * 3 + 1.5 * (a + 1) + 2.0
            agenda.at(when, lambda k=k, a=a: yw_hop(k, a))
    drain(wgu.at[pl.ds(0, 3584), pl.ds(0, 128)], s_yw[0])
    drain(wgu.at[pl.ds(0, 3584), pl.ds(128, 128)], s_yw[1])
    drain(wd.at[pl.ds(0, 7)], s_yw[2])

    s_co, s_cb = new_send(), new_send()
    r_co = {z: new_recv() for z in range(1, 8)}
    r_cb = new_recv()

    def coef_start():
        for z in range(1, 8):
            send(coef.at[0, 0], coef.at[0, Z_POS[8 - z]], s_co, r_co[8 - z], z_dev(z))

    def coef_mirror():
        for z in range(1, 8):
            wait_recv(coef.at[0, Z_POS[z]], r_co[z])
        send(coef.at[0], coef.at[1], s_cb, r_cb, sib)

    agenda.at(4.0, coef_start)
    agenda.at(16.0, coef_mirror)
    drain(coef.at[0, pl.ds(0, 7)], s_co)
    drain(coef.at[0], s_cb)

    t_tok = gather(tok, 0.0)
    t_dout0 = 15.0
    t_dout = gather(dout, t_dout0)

    def weight_wait():
        for copy in later:
            copy.wait()

    agenda.at(t_tok + 0.01, weight_wait)
    s_hid = [new_send() for _ in range(2)]
    r_hid = {(d, i): new_recv() for d in (1, 2, 3) for i in range(2)}
    own_cols = pl.ds(pl.multiple_of(xo * 128, 128), 128)

    def project(buf, w, r0, n, out):
        out[pl.ds(r0, n), :] = jnp.dot(
            buf[0, pl.ds(r0, n), :],
            w[pl.ds(pl.multiple_of(xo * 1024, 1024), 1024), :],
            preferred_element_type=F32,
        )

        @pl.loop(1, 4)
        def _(rel):
            chunk = lax.rem(xo + rel, 4)
            out[pl.ds(r0, n), :] += jnp.dot(
                buf[rel, pl.ds(r0, n), :],
                w[pl.ds(pl.multiple_of(chunk * 1024, 1024), 1024), :],
                preferred_element_type=F32,
            )

    def teacher_hidden(i):
        r0 = 256 * (1 - i)
        project(tok, wt, r0, 256, gu)
        gate = gu[pl.ds(r0, 256), 0:128]
        up = gu[pl.ds(r0, 256), 128:256]
        hid[pl.ds(r0, 256), own_cols] = (gate * sigmoid(gate) * up).astype(BF16)
        ref = hid.at[pl.ds(r0, 256), own_cols]
        for d in (1, 3, 2):
            send(ref, ref, s_hid[i], r_hid[4 - d, i], x_dev(d))

    t_hid = t_tok + 0.02
    agenda.at(t_hid, lambda: teacher_hidden(0))
    agenda.at(t_hid + 1.2, lambda: teacher_hidden(1))
    for i in range(2):
        drain(hid.at[pl.ds(0, 256), pl.ds(0, 384)], s_hid[i])

    s_sp = new_send()
    r_sp = new_recv()
    s_rs = new_send()
    r_rs = {z: new_recv() for z in range(1, 8)}

    def coef_column(other, half):
        lanes = lax.broadcasted_iota(jnp.int32, (128, 128), 1)
        rows = coef[other].astype(F32).reshape(128, 128)
        wanted = (lanes == half * 16 + eo) | (lanes == 32 + half * 16 + eo)
        return jnp.sum(jnp.where(wanted, rows, 0.0), axis=1, keepdims=True)

    def teacher_down(i):
        other = 1 - i
        r0 = 256 * other
        for d in (1, 3, 2):
            cols = pl.ds(pl.multiple_of(lax.rem(xo + d, 4) * 128, 128), 128)
            wait_recv(hid.at[pl.ds(r0, 256), cols], r_hid[d, i])
        if i == 0:
            wait_recv(coef.at[1], r_cb)
        if i == 1:
            wait_recv(sibp, r_sp)
        for half in range(2):
            scale = coef_column(other, half)
            for q in range(2):
                cols = slice(q * 512, q * 512 + 512)
                res = jnp.dot(
                    hid[pl.ds(r0 + half * 128, 128), :], wed[:, cols], preferred_element_type=F32
                )
                res = res * scale
                if i == 1:
                    res = res + sibp[half, :, cols].astype(F32)
                part[other, half, :, cols] = res.astype(BF16)
        if i == 0:
            send(part.at[1], sibp, s_sp, r_sp, sib)
        else:
            for z in (4, 3, 5, 2, 6, 1, 7):
                rows = pl.ds(Z_POS[z] * 16, 16)
                send(part.at[0, :, rows], rsb.at[8 - z], s_rs, r_rs[8 - z], z_dev(z))

    t_down = t_hid + 6.0
    agenda.at(t_down, lambda: teacher_down(0))
    agenda.at(t_down + 3.5, lambda: teacher_down(1))
    drain(part.at[1], s_sp)
    drain(part.at[0, :, pl.ds(16, 112)], s_rs)

    def teacher_sum():
        for z in range(1, 8):
            wait_recv(rsb.at[z], r_rs[z])
        for half in range(2):
            total = part[0, half, 0:16, :].astype(F32)
            for z in range(1, 8):
                total = total + rsb[z, half].astype(F32)
            row = total.astype(BF16)
            t_out[half * 16 : half * 16 + 16, :] = row
            act[0, half * 128 : half * 128 + 16, :] = row

    t_sum = t_down + 3.5 + 14.0
    agenda.at(t_sum, teacher_sum)

    def student_back():
        hg[...] = jnp.zeros_like(hg)

        @pl.loop(0, 4)
        def _(rel):
            chunk = lax.rem(xo + rel, 4)
            for j in range(2):
                hg[...] += lax.dot_general(
                    dout[rel, :, j * 512 : j * 512 + 512],
                    wd[chunk * 2 + j],
                    (((1,), (1,)), ((), ())),
                    preferred_element_type=F32,
                )

    agenda.at(max(t_dout + 0.1, 35.5), student_back)
    t_act = gather(act, t_sum + 0.1)

    def student_rows(i):
        r0 = 256 * i
        project(act, wgu, r0, 256, gu)
        gate = gu[pl.ds(r0, 256), 0:128]
        up = gu[pl.ds(r0, 256), 128:256]
        back = hg[pl.ds(r0, 256), :]
        sig = sigmoid(gate)
        silu = gate * sig
        cols = slice(r0, r0 + 256)
        gt[0:128, cols] = (back * up * (sig * (1.0 + gate * (1.0 - sig)))).T.astype(BF16)
        gt[128:256, cols] = (back * silu).T.astype(BF16)
        gt[256:384, cols] = (silu * up).T.astype(BF16)

    agenda.at(t_act + 0.1, lambda: student_rows(0))
    agenda.at(t_act + 0.2, lambda: student_rows(1))

    s_yg = [new_send() for _ in range(3)]
    r_yg = {(d, k, a): new_recv() for d in "RL" for k in range(4) for a in range(3)}

    def term(k, a):
        owner = lax.rem(yo + k, 8)
        rel = lax.rem(owner // 2 - xo + 4, 4)
        cols = pl.ds(pl.multiple_of(lax.rem(owner, 2) * 512, 512), 512)
        if a == 0:
            grad[k, 0:256, :] = jnp.dot(
                gt[0:256, :], act[rel, :, cols], preferred_element_type=F32
            ).astype(BF16)
        else:
            grad[k, 256:384, :] = jnp.dot(
                gt[256:384, :], dout[rel, :, cols], preferred_element_type=F32
            ).astype(BF16)

    def yg_ref(d, k, a):
        if k == 0:
            return ring.at[0 if d == "R" else 1, 0, a, pl.ds(0 if d == "R" else 64, 64)]
        return ring.at[0 if d == "R" else 1, k, a]

    def yg_send(d, k, a):
        if k == 0:
            src = grad.at[4, pl.ds(a * 128 + (0 if d == "R" else 64), 64)]
        else:
            src = grad.at[4 - k if d == "R" else 4 + k, pl.ds(a * 128, 128)]
        send(src, yg_ref(d, k, a), s_yg[a], r_yg[d, k, a], y_dev(1 if d == "R" else -1))

    t_g = t_act + 1.0

    def first_terms():
        term(4, 0)
        for a in range(2):
            for d in "RL":
                yg_send(d, 0, a)
        term(4, 1)
        for d in "RL":
            yg_send(d, 0, 2)
        for k in (3, 5):
            for a in range(2):
                term(k, a)

    agenda.at(t_g, first_terms)
    for i, k in enumerate((2, 6, 1, 7, 0)):
        for a in range(2):
            agenda.at(t_g + 8.0 + 3.2 * i + 1.5 * a, lambda k=k, a=a: term(k, a))

    def yg_hop(k, a):
        for d in "RL":
            wait_recv(yg_ref(d, k - 1, a), r_yg[d, k - 1, a])
            way = 0 if d == "R" else 1
            mine = 4 - k if d == "R" else 4 + k
            lo, n = a * 128, 128
            off = 0
            if k == 1:
                off, n = (0, 64) if d == "R" else (64, 64)
            grad[mine, lo + off : lo + off + n, :] = (
                grad[mine, lo + off : lo + off + n, :].astype(F32)
                + ring[way, k - 1, a, off : off + n, :].astype(F32)
            ).astype(BF16)
            yg_send(d, k, a)

    for k in range(1, 4):
        for a in range(3):
            agenda.at(t_g + 3.0 + 8.9 * (k - 1) + 2.95 * a, lambda k=k, a=a: yg_hop(k, a))

    def yg_last(a):
        for d in "RL":
            wait_recv(yg_ref(d, 3, a), r_yg[d, 3, a])
        total = (
            grad[0, a * 128 : a * 128 + 128, :].astype(F32)
            + ring[0, 3, a].astype(F32)
            + ring[1, 3, a].astype(F32)
        )
        if a == 0:
            gg_out[...] = total.T
        elif a == 1:
            gu_out[...] = total.T
        else:
            gd_out[...] = total

    for a in range(3):
        agenda.at(t_g + 3.0 + 8.9 * 3 + 2.95 * a, lambda a=a: yg_last(a))
        drain(grad.at[pl.ds(1, 7), pl.ds(a * 128, 128)], s_yg[a])

    agenda.run()
    for step in drains:
        step()


def body(*args):
    any_spec = pl.BlockSpec(memory_space=pl.ANY)
    vmem = pl.BlockSpec(memory_space=pltpu.VMEM)
    scratch = [
        pltpu.VMEM((4, 512, 1024), BF16),
        pltpu.VMEM((4, 512, 1024), BF16),
        pltpu.VMEM((4, 512, 1024), BF16),
        pltpu.VMEM((4096, 256), BF16),
        pltpu.VMEM((512, 1024), BF16),
        pltpu.VMEM((4096, 256), BF16),
        pltpu.VMEM((8, 128, 512), BF16),
        pltpu.VMEM((512, 512), BF16),
        pltpu.VMEM((2, 8, 16, 128), BF16),
        pltpu.VMEM((2, 2, 128, 1024), BF16),
        pltpu.VMEM((2, 128, 1024), BF16),
        pltpu.VMEM((8, 2, 16, 1024), BF16),
        pltpu.VMEM((512, 256), F32),
        pltpu.VMEM((512, 128), F32),
        pltpu.VMEM((384, 512), BF16),
        pltpu.VMEM((8, 384, 512), BF16),
        pltpu.VMEM((2, 4, 3, 128, 512), BF16),
        pltpu.SemaphoreType.DMA((N_SEND,)),
        pltpu.SemaphoreType.DMA((N_RECV,)),
        pltpu.SemaphoreType.DMA((10,)),
    ]
    return pl.pallas_call(
        kernel,
        out_shape=(
            jax.ShapeDtypeStruct((32, 1024), BF16),
            jax.ShapeDtypeStruct((512, 128), F32),
            jax.ShapeDtypeStruct((512, 128), F32),
            jax.ShapeDtypeStruct((128, 512), F32),
        ),
        in_specs=[any_spec, vmem, vmem] + [any_spec] * 7,
        out_specs=(vmem,) * 4,
        scratch_shapes=scratch,
        compiler_params=pltpu.CompilerParams(
            collective_id=1, has_side_effects=True, vmem_limit_bytes=52 * 1024 * 1024
        ),
        cost_estimate=pl.CostEstimate(flops=5_000_000_000, bytes_accessed=12_000_000, transcendentals=400_000),
        name="distill_window",
    )(*args)


def solution(mesh):
    in_specs = (
        P(("seq", "exp"), "tp"),
        P(("seq", "exp"), None),
        P(("seq", "exp"), None),
        P("exp", None, "tp"),
        P("exp", None, "tp"),
        P("exp", None, "tp"),
        P("seq", ("exp", "tp")),
        P("seq", ("exp", "tp")),
        P(("exp", "tp"), "seq"),
        P(("seq", "exp"), "tp"),
    )
    out_specs = (
        P(("seq", "exp"), "tp"),
        P("seq", ("exp", "tp")),
        P("seq", ("exp", "tp")),
        P(("exp", "tp"), "seq"),
    )
    return jax.shard_map(body, mesh=mesh, in_specs=in_specs, out_specs=out_specs, check_vma=False)
```

time: 445 us -> 138 us (0.31)
  waiting for transfers between devices: 313 us -> 0 us
  Pallas kernels: 0 us -> 129 us
  blocking collectives: 67.1 us -> 0 us
  matrix products: 29.6 us -> 0 us
  between operations: 14 us -> 0.66 us
  starting transfers between devices: 11.4 us -> 0 us
  local copies, waits for them, and re-layouts: 0.19 us -> 7.98 us
  other arithmetic: 5.8 us -> 0 us
    all_gather x6 -> x0, waiting for transfers between devices: 174 us -> none  [the longest x1 51.7 us: body(): lax.all_gather(wide_act, 'exp', axis=0, tiled=True)]
    pallas_call x0 -> x1, Pallas kernels: none -> 129 us  [body(): pl.pallas_call(kernel, out_shape=(jax.ShapeDtypeStruct((32, 1024), BF16),...]
    reduce_scatter x3 -> x0, waiting for transfers between devices: 115 us -> none  [the longest x1 41.4 us: body(): lax.psum_scatter(down_term.astype(jnp.bfloat16), 'seq', scatter_dimension...]
    all_to_all x1 -> x0, blocking collectives: 34.7 us -> none  [body(): lax.all_to_all(outgoing, 'exp', split_axis=0, concat_axis=0, tiled=True)]
    all_gather x3 -> x0, blocking collectives: 32.4 us -> none  [the longest x1 12.4 us: body(): lax.all_gather(out_grad, 'tp', axis=1, tiled=True)]
    dot_general x11 -> x0, matrix products: 29.6 us -> none  [the longest x1 4.51 us: body(): lax.dot_general(act_rows, up_grad, contract_rows, preferred_element_type=...]
    all_to_all x1 -> x0, waiting for transfers between devices: 22.6 us -> none  [body(): lax.all_to_all(expert_out.astype(jnp.bfloat16), 'exp', split_axis=0, conc...]
    all_to_all x1 -> x0, starting transfers between devices: 11 us -> none  [body(): lax.all_to_all(expert_out.astype(jnp.bfloat16), 'exp', split_axis=0, conc...]
  transfers between devices with their start and end apart: 10 -> 0, of which waited for: 9 -> 0; matrix products, arithmetic and copies ran while one was open for 6% -> 0% of each run, Pallas kernels for 0% -> 0%
where the time goes in v1:
time: 138 us
  Pallas kernels  129 us (93%)
  local copies, waits for them, and re-layouts  7.98 us (6%)
    pallas_call x1, Pallas kernels, body(): pl.pallas_call(kernel, out_shape=(jax.ShapeDtypeStruct((32, 1024), BF16),...  129 us
    unnamed x18, local copies, waits for them, and re-layouts  7.98 us

profile of v1, /device:TPU:1, one launch (start us, length us, event | category | flops | bytes accessed | tf_op | source)
XLA Modules:
  0.0 137.8 jit_solution(8762380036126992193)
XLA Ops:
  0.6 0.0 copy-start.5
  0.6 0.8 copy.14.ids
  1.4 0.0 copy-done.5
  1.4 0.1 copy.15.weights
  1.5 0.0 copy-start
  1.5 0.9 copy-done
  2.4 0.0 copy-start.1
  2.4 0.9 copy-done.1
  3.3 0.0 copy-start.2
  3.3 0.9 copy-done.2
  4.2 0.0 copy-start.3
  4.2 0.8 copy-done.3
  5.0 0.0 copy-start.4
  5.0 0.8 copy-done.4
  5.9 129.2 %distill_window.1 = (bf16[32,1024]{1,0:T(8,128)(2,1)S(1)}, f32[512,128]{1,0:T(8,128)S(1)}, f32[512,128]{1,0:T(8,128)S(1)}, f32[128,512]{1,0:T(8,128)S(1)}) custom-call(bf16[32,1024]{1,0:T(8,128)(2,1)S(1)} %copy-done.3, s32[32,8]{1,0:T(8,128)S(1)} %copy.14.ids, f32[32,8]{1,0:T(8,128)S(1)} %copy.15.weights, bf16[1,4096,128]{2,1,0:T(8,128)(2,1)} %egate.1, ...), custom_call_target="tpu_custom_call" | custom-call | flops 5000000000 | bytes 12000000 | tf_op jit(solution)/shard_map/distill_window/pallas_call | solution.py:573
  135.1 0.6 copy.20
  135.7 0.7 copy.21
  136.4 0.7 copy.22
  137.1 0.7 copy.23
Async XLA Ops:
  0.6 0.8 copy-start.5
  1.5 0.9 copy-start
  2.4 0.9 copy-start.1
  3.3 0.9 copy-start.2
  4.2 0.8 copy-start.3
  5.0 0.8 copy-start.4

commit v2 on v1

v2 whole, which is shorter than its diff:
```python
import jax
import jax.numpy as jnp
from jax import lax
from jax.experimental import pallas as pl
from jax.experimental.pallas import tpu as pltpu
from jax.sharding import PartitionSpec as P

MESH = pl.DeviceIdType.MESH
F32 = jnp.float32
BF16 = jnp.bfloat16
Z_ORDER = (0, 1, 7, 2, 6, 3, 5, 4)
Z_POS = {z: i for i, z in enumerate(Z_ORDER)}
N_RECV = 400
N_SEND = 96


WAVES = ((0, 160), (320, 96))
Z_FIRST = 640


def row_at(pos, other=0):
    return other * 160 + pos * 32 if pos < 5 else 320 + other * 96 + (pos - 5) * 32


def row_of(z, other=0):
    return row_at(Z_POS[z % 8], other)


def sigmoid(a):
    return 1.0 / (1.0 + jnp.exp(-a))


class Agenda:
    def __init__(self):
        self.steps = []

    def at(self, time, step):
        self.steps.append((time, len(self.steps), step))

    def run(self):
        for _, _, step in sorted(self.steps, key=lambda s: (s[0], s[1])):
            step()


def kernel(
    tokens, ids, weights, egate, eup, edown, sgate, sup, sdown, ograd,
    t_hbm, gg_hbm, gu_hbm, gd_hbm,
    tok, act, dout, wt, wed, wgu, wd, hid, coef, part, sibp, rsb, gu, hg, gt, grad, ring, t_out, gg_out, gu_out, gd_out,
    send_sems, recv_sems, local_sems,
):
    yo = lax.axis_index("seq")
    eo = lax.axis_index("exp")
    xo = lax.axis_index("tp")
    zo = eo // 2
    co = lax.rem(eo, 2)

    def z_dev(d):
        return (yo, lax.rem(zo + d + 8, 8) * 2 + co, xo)

    def x_dev(d):
        return (yo, eo, lax.rem(xo + d + 4, 4))

    def y_dev(d):
        return (lax.rem(yo + d + 8, 8), eo, xo)

    sib = (yo, zo * 2 + (1 - co), xo)
    agenda = Agenda()
    drains = []
    counts = {"send": 0, "recv": 0, "local": 0}

    def new_send():
        counts["send"] += 1
        assert counts["send"] <= N_SEND
        return send_sems.at[counts["send"] - 1]

    def new_recv():
        counts["recv"] += 1
        assert counts["recv"] <= N_RECV
        return recv_sems.at[counts["recv"] - 1]

    def send(src, dst, s_sem, r_sem, device):
        pltpu.make_async_remote_copy(
            src_ref=src, dst_ref=dst, send_sem=s_sem, recv_sem=r_sem,
            device_id=device, device_id_type=MESH,
        ).start()

    def wait_recv(ref, r_sem):
        pltpu.make_async_remote_copy(
            src_ref=ref, dst_ref=ref, send_sem=send_sems.at[0], recv_sem=r_sem,
            device_id=sib, device_id_type=MESH,
        ).wait_recv()

    def drain(ref, s_sem):
        def step():
            pltpu.make_async_remote_copy(
                src_ref=ref, dst_ref=ref, send_sem=s_sem, recv_sem=recv_sems.at[0],
                device_id=sib, device_id_type=MESH,
            ).wait_send()

        drains.append(step)

    local = []

    def load(src, dst):
        copy = pltpu.make_async_copy(src, dst, local_sems.at[len(local)])
        copy.start()
        local.append(copy)
        return copy

    first = [
        load(tokens, tok.at[0, pl.ds(0, 32)]),
        load(sgate, wgu.at[pl.ds(pl.multiple_of(yo * 512, 512), 512), pl.ds(0, 128)]),
        load(sup, wgu.at[pl.ds(pl.multiple_of(yo * 512, 512), 512), pl.ds(128, 128)]),
        load(sdown, wd.at[yo]),
        load(ograd, dout.at[0, pl.ds(0, 32)]),
    ]
    stores = []

    def store(i, src, dst):
        copy = pltpu.make_async_copy(src, dst, local_sems.at[8 + i])
        copy.start()
        stores.append(copy)

    later = [
        load(egate.at[0], wt.at[:, pl.ds(0, 128)]),
        load(eup.at[0], wt.at[:, pl.ds(128, 128)]),
        load(edown.at[0], wed),
    ]

    barrier = pltpu.get_barrier_semaphore()
    peers = [z_dev(d) for d in range(1, 8)] + [x_dev(d) for d in range(1, 4)] + [y_dev(1), y_dev(-1), sib]
    for device in peers:
        pl.semaphore_signal(barrier, inc=1, device_id=device, device_id_type=MESH)

    lane = lax.broadcasted_iota(jnp.int32, (16, 128), 1)
    lane_e = lax.rem(lane, 16)
    lane_half = lax.rem(lane // 16, 2)
    blank = jnp.zeros((8, 96), jnp.int32)
    names = jnp.concatenate([ids[...], blank], axis=1).T
    shares = jnp.concatenate([weights[...], blank.astype(F32)], axis=1).T
    halves = []
    for half in range(2):
        total = jnp.zeros((16, 128), F32)
        for k in range(8):
            name = names[half * 16 : half * 16 + 16, k : k + 1]
            weight = shares[half * 16 : half * 16 + 16, k : k + 1]
            total = total + jnp.where(lane_e == name, weight, 0.0)
        halves.append(total)
    value = jnp.where(lane_half == 0, halves[0], halves[1])
    high = value.astype(BF16).astype(F32)
    value = jnp.where(lane < 32, high, jnp.where(lane < 64, value - high, 0.0))
    coef[0, 0] = value.astype(BF16)

    pl.semaphore_wait(barrier, len(peers))
    for copy in first:
        copy.wait()

    def gather(buf, t0, times=None):
        s_z0, s_x0, s_f0, s_b0 = new_send(), [new_send() for _ in range(2)], new_send(), new_send()
        s_x2, s_x1, s_z1, s_b1 = new_send(), new_send(), new_send(), new_send()
        pieces = ((0, 1), (1, 2), (3, 2), (5, 2), (7, 1))
        r_z0 = {(d, k): new_recv() for d in "RL" for k in range(1, 5)}
        r_x0 = {(rel, k): new_recv() for rel in (1, 3) for k in range(5)}
        r_f0 = {(rel, k): new_recv() for rel in (1, 3) for k in range(4)}
        r_x2 = new_recv()
        r_x1 = {rel: new_recv() for rel in (1, 2, 3)}
        r_z1 = {(d, k, c): new_recv() for d in "RL" for k in range(1, 5) for c in range(4)}
        r_b0, r_b1 = [new_recv() for _ in range(2)], [new_recv() for _ in range(2)]
        step_dev = {"R": z_dev(1), "L": z_dev(-1)}
        cols0, cols1 = pl.ds(0, Z_FIRST), pl.ds(Z_FIRST, 1024 - Z_FIRST)
        part_cols = {"R": pl.ds(0, 384), "L": pl.ds(384, Z_FIRST - 384)}

        def came(d, k):
            return (8 - k) % 8 if d == "R" else k % 8

        def z0_ref(z, d, k):
            return buf.at[0, pl.ds(row_of(z), 32), part_cols[d] if k == 4 else cols0]

        def z0_send(d, k):
            send(z0_ref(came(d, k - 1), d, k), z0_ref(came(d, k), d, k), s_z0, r_z0[d, k], step_dev[d])

        def piece_ref(rel, k, cols=cols0, other=0):
            pos, n = pieces[k]
            return buf.at[rel, pl.ds(row_at(pos, other), 32 * n), cols]

        def x0_piece(k):
            for i, d in enumerate((1, -1)):
                send(piece_ref(0, k), piece_ref((-d) % 4, k), s_x0[i], r_x0[(-d) % 4, k], x_dev(d))
            if k == 4:
                send(piece_ref(0, k), piece_ref(2, k), s_x2, r_x2, x_dev(2))

        def z1_ref(z, c):
            return buf.at[c, pl.ds(row_of(z), 32), cols1]

        def z1_send(d, k, c):
            send(z1_ref(came(d, k - 1), c), z1_ref(came(d, k), c), s_z1, r_z1[d, k, c], step_dev[d])

        def b0_send(rel, k):
            send(piece_ref(rel, k), piece_ref(rel, k, other=1), s_b0, r_b0[0 if k < 3 else 1], sib)

        def b1_send(z):
            send(
                buf.at[:, pl.ds(row_of(z), 32), cols1],
                buf.at[:, pl.ds(row_of(z, 1), 32), cols1],
                s_b1, r_b1[0 if Z_POS[z] < 5 else 1], sib,
            )

        plan = {("begin",): 0.0, ("ready", 0): 13.5, ("ready", 1): 16.6}
        for k, (there, beyond) in enumerate(((3.1, 11.0), (6.8, 11.5), (9.8, 12.3), (12.7, 15.4), (14.6, 15.5))):
            plan["x0", k] = 2.9 * k + 0.01
            plan["x0_done", k], plan["f0_done", k] = there, beyond
        plan["x1",] = 2.95
        for k in range(1, 5):
            plan["z0", k] = 2.9 * k
            for c, when in ((0, 0.2), (1, 2.5), (3, 3.0), (2, 3.5)):
                plan["z1", k, c] = 2.9 * k + when
        plan.update(times or {})

        def at(name, step):
            agenda.at(t0 + plan[name], step)

        def begin():
            for d in "RL":
                z0_send(d, 1)
            for d in (1, -1, 2):
                send(z1_ref(0, 0), z1_ref(0, (-d) % 4), s_x1, r_x1[(-d) % 4], x_dev(d))
            for d in "RL":
                z1_send(d, 1, 0)

        at(("begin",), begin)

        def z0_hop(k):
            for d in "RL":
                wait_recv(z0_ref(came(d, k), d, k), r_z0[d, k])
                if k < 4:
                    z0_send(d, k + 1)

        def x0_start(k):
            x0_piece(k)
            b0_send(0, k)

        for k in range(1, 5):
            at(("z0", k), lambda k=k: z0_hop(k))
        for k in range(5):
            at(("x0", k), lambda k=k: x0_start(k))

        def x0_done(rel, k):
            wait_recv(piece_ref(rel, k), r_x0[rel, k])
            if k < 4:
                d, way = (1, "R") if rel == 3 else (-1, "L")
                send(
                    piece_ref(rel, k, part_cols[way]), piece_ref(2, k, part_cols[way]),
                    s_f0, r_f0[rel, k], x_dev(d),
                )
            b0_send(rel, k)

        def f0_done(k):
            if k == 4:
                wait_recv(piece_ref(2, k), r_x2)
            else:
                for rel, way in ((3, "R"), (1, "L")):
                    wait_recv(piece_ref(2, k, part_cols[way]), r_f0[rel, k])
            b0_send(2, k)

        for k in range(5):
            for rel in (1, 3):
                at(("x0_done", k), lambda rel=rel, k=k: x0_done(rel, k))
            at(("f0_done", k), lambda k=k: f0_done(k))

        def x1_done(rel):
            wait_recv(z1_ref(0, rel), r_x1[rel])
            for d in "RL":
                z1_send(d, 1, rel)
            if rel == 2:
                b1_send(0)

        for rel in (1, 3, 2):
            at(("x1",), lambda rel=rel: x1_done(rel))

        def z1_hop(k, c):
            for d in "RL":
                if k == 4 and (d == "R") != (c in (0, 1)):
                    continue
                z = came(d, k)
                wait_recv(z1_ref(z, c), r_z1[d, k, c])
                if k < 3 or (k == 3 and (d == "R") == (c in (0, 1))):
                    z1_send(d, k + 1, c)
                if c == 2:
                    b1_send(z)

        for k in range(1, 5):
            for c in (0, 1, 3, 2):
                at(("z1", k, c), lambda k=k, c=c: z1_hop(k, c))

        def finish(wave):
            first, n = WAVES[wave]
            rows = pl.ds(first + n, n)
            wait_recv(buf.at[:, rows, cols0], r_b0[wave])
            wait_recv(buf.at[:, rows, cols1], r_b1[wave])

        for wave in range(2):
            at(("ready", wave), lambda wave=wave: finish(wave))
        drain(buf.at[0, pl.ds(0, 224), cols0], s_z0)
        for sem in s_x0:
            drain(buf.at[0, pl.ds(0, 256), cols0], sem)
        drain(buf.at[0, pl.ds(0, 224), cols0], s_f0)
        drain(buf.at[0, pl.ds(0, 32), cols0], s_x2)
        drain(buf.at[:, pl.ds(0, 256), cols0], s_b0)
        drain(buf.at[pl.ds(1, 3), pl.ds(0, 32), cols1], s_x1)
        drain(buf.at[:, pl.ds(0, 224), cols1], s_z1)
        drain(buf.at[:, pl.ds(0, 256), cols1], s_b1)
        return [t0 + plan["ready", 0], t0 + plan["ready", 1]]

    s_yw = [new_send() for _ in range(3)]
    r_yw = {(d, k, a): new_recv() for d in "RL" for k in range(1, 5) for a in range(3)}

    def yw_ref(a, origin, d, k):
        if a < 2:
            start, n = origin * 512, 512
            if k == 4:
                start, n = start + (0 if d == "R" else 256), 256
            return wgu.at[pl.ds(pl.multiple_of(start, 256), n), pl.ds(a * 128, 128)]
        if k == 4:
            return wd.at[origin, pl.ds(0 if d == "R" else 64, 64)]
        return wd.at[origin]

    def yw_origin(d, k):
        return lax.rem(yo + (8 - k if d == "R" else k), 8)

    def yw_send(d, k, a):
        ref = yw_ref(a, yw_origin(d, k - 1), d, k)
        send(ref, ref, s_yw[a], r_yw[d, k, a], y_dev(1 if d == "R" else -1))

    def yw_start():
        for a in range(3):
            for d in "RL":
                yw_send(d, 1, a)

    def yw_hop(k, a):
        for d in "RL":
            wait_recv(yw_ref(a, yw_origin(d, k), d, k), r_yw[d, k, a])
            if k < 4:
                yw_send(d, k + 1, a)

    agenda.at(0.01, yw_start)
    for k in range(1, 5):
        for a in range(3):
            when = 8.9 * (k - 1) + 2.95 * (a + 1) + 2.0 if k < 4 else 8.9 * 3 + 1.5 * (a + 1) + 2.0
            agenda.at(1.25 * when + 2.0, lambda k=k, a=a: yw_hop(k, a))
    drain(wgu.at[pl.ds(0, 3584), pl.ds(0, 128)], s_yw[0])
    drain(wgu.at[pl.ds(0, 3584), pl.ds(128, 128)], s_yw[1])
    drain(wd.at[pl.ds(0, 7)], s_yw[2])

    s_co, s_cb = new_send(), new_send()
    r_co = {z: new_recv() for z in range(1, 8)}
    r_cb = new_recv()

    def coef_start():
        for z in range(1, 8):
            send(coef.at[0, 0], coef.at[0, Z_POS[8 - z]], s_co, r_co[8 - z], z_dev(z))

    def coef_mirror():
        for z in range(1, 8):
            wait_recv(coef.at[0, Z_POS[z]], r_co[z])
        send(coef.at[0], coef.at[1], s_cb, r_cb, sib)

    agenda.at(4.0, coef_start)
    agenda.at(16.0, coef_mirror)
    drain(coef.at[0, pl.ds(0, 7)], s_co)
    drain(coef.at[0], s_cb)

    t_tok = gather(tok, 0.0)
    late = {("begin",): 11.0, ("x1",): 15.1, ("ready", 0): 31.0, ("ready", 1): 32.0}
    for k, (when, start, there, beyond) in enumerate(
        ((0, 18.3, 22.5, 27.0), (15.2, 18.4, 24.2, 28.0), (18.2, 20.7, 25.9, 29.0), (20.6, 22.6, 26.5, 30.0), (26.0, 26.1, 30.0, 30.1))
    ):
        late["x0", k], late["x0_done", k], late["f0_done", k] = start, there, beyond
        if k:
            late["z0", k] = when
            for c in range(4):
                late["z1", k, c] = when + (0.1 if k < 3 else 2.0 if k == 3 else 0.4)
    gather(dout, 0.0, late)

    def weight_wait():
        for copy in later:
            copy.wait()

    agenda.at(t_tok[0] + 0.01, weight_wait)
    s_hid = [new_send() for _ in range(2)]
    r_hid = {(d, w): new_recv() for d in (1, 2, 3) for w in range(2)}

    def hid_cols(d):
        return pl.ds(pl.multiple_of(lax.rem(xo + d, 4) * 128, 128), 128)

    def project(buf, w, rows, out):
        out[rows, :] = jnp.dot(
            buf[0, rows, :],
            w[pl.ds(pl.multiple_of(xo * 1024, 1024), 1024), :],
            preferred_element_type=F32,
        )

        @pl.loop(1, 4)
        def _(rel):
            chunk = lax.rem(xo + rel, 4)
            out[rows, :] += jnp.dot(
                buf[rel, rows, :],
                w[pl.ds(pl.multiple_of(chunk * 1024, 1024), 1024), :],
                preferred_element_type=F32,
            )

    def wave_rows(wave):
        first, n = WAVES[wave]
        return pl.ds(first, 2 * n)

    def teacher_hidden(wave):
        rows = wave_rows(wave)
        project(tok, wt, rows, gu)
        gate = gu[rows, 0:128]
        up = gu[rows, 128:256]
        hid[rows, hid_cols(0)] = (gate * sigmoid(gate) * up).astype(BF16)
        ref = hid.at[rows, hid_cols(0)]
        for d in (1, 3, 2):
            send(ref, ref, s_hid[wave], r_hid[4 - d, wave], x_dev(d))

    for wave in range(2):
        agenda.at(t_tok[wave] + 0.02, lambda wave=wave: teacher_hidden(wave))
        drain(hid.at[wave_rows(wave), pl.ds(0, 384)], s_hid[wave])

    s_sp = [new_send() for _ in range(2)]
    r_sp = [new_recv() for _ in range(2)]
    s_rs = new_send()
    r_rs = {z: new_recv() for z in range(1, 8)}

    def coef_column(other, wave):
        start, n = ((0, 5), (5, 3))[wave]
        lanes = lax.broadcasted_iota(jnp.int32, (n, 16, 128), 2)
        rows = coef[other, start : start + n].astype(F32)
        cols = []
        for half in range(2):
            wanted = (lanes == half * 16 + eo) | (lanes == 32 + half * 16 + eo)
            cols.append(jnp.sum(jnp.where(wanted, rows, 0.0), axis=2, keepdims=True))
        return jnp.concatenate(cols, axis=1).reshape(n * 32, 1)

    def hid_wait(wave):
        for d in (1, 3, 2):
            wait_recv(hid.at[wave_rows(wave), hid_cols(d)], r_hid[d, wave])
        if wave == 0:
            wait_recv(coef.at[1], r_cb)

    def teacher_down(wave, other):
        first, n = WAVES[wave]
        rows = pl.ds(first + other * n, n)
        own = pl.ds(first, n)
        scale = coef_column(other, wave)
        if other == 0:
            wait_recv(sibp.at[own], r_sp[wave])
        for q in range(2):
            cols = slice(q * 512, q * 512 + 512)
            res = jnp.dot(hid[rows, :], wed[:, cols], preferred_element_type=F32) * scale
            if other == 0:
                res = res + sibp[own, cols].astype(F32)
            part[rows, cols] = res.astype(BF16)
        if other == 1:
            send(part.at[rows], sibp.at[own], s_sp[wave], r_sp[wave], sib)
        else:
            for z in ((2, 6, 1, 7), (4, 3, 5))[wave]:
                send(part.at[pl.ds(row_of(z), 32)], rsb.at[8 - z], s_rs, r_rs[8 - z], z_dev(z))

    t_down = [20.2, 22.9]
    for wave in range(2):
        agenda.at(t_down[wave], lambda wave=wave: hid_wait(wave))
        for other in (1, 0):
            agenda.at(
                t_down[wave] + (0.1, 2.1)[1 - other],
                lambda wave=wave, other=other: teacher_down(wave, other),
            )
        first, n = WAVES[wave]
        drain(part.at[pl.ds(first + n, n)], s_sp[wave])
    drain(part.at[pl.ds(0, 224)], s_rs)

    def teacher_sum():
        total = part[0:32, :].astype(F32)
        for z in (1, 7, 2, 6, 3, 5, 4):
            wait_recv(rsb.at[z], r_rs[z])
        for z in range(1, 8):
            total = total + rsb[z].astype(F32)
        row = total.astype(BF16)
        t_out[...] = row
        store(0, t_out, t_hbm)
        act[0, 0:32, :] = row

    t_sum = 35.0
    agenda.at(t_sum, teacher_sum)

    def student_back(rel):
        chunk = lax.rem(xo + rel, 4)
        total = jnp.zeros((512, 128), F32) if rel == 0 else hg[...]
        for j in range(2):
            total = total + lax.dot_general(
                dout[rel, :, j * 512 : j * 512 + 512],
                wd[chunk * 2 + j],
                (((1,), (1,)), ((), ())),
                preferred_element_type=F32,
            )
        hg[...] = total

    t_act = gather(act, t_sum + 0.1)
    for rel, when in enumerate((1.0, 4.0, 7.0, 10.0)):
        agenda.at(max(45.5, t_sum + 0.1 + when), lambda rel=rel: student_back(rel))

    def student_rows(wave):
        first, n = WAVES[wave]
        rows = pl.ds(first, 2 * n)
        project(act, wgu, rows, gu)
        gate = gu[rows, 0:128]
        up = gu[rows, 128:256]
        back = hg[rows, :]
        sig = sigmoid(gate)
        silu = gate * sig
        terms = (back * up * (sig * (1.0 + gate * (1.0 - sig))), back * silu, silu * up)
        for i, term in enumerate(terms):
            gt[i * 128 : i * 128 + 128, rows] = term.T.astype(BF16)

    for wave in range(2):
        agenda.at(t_act[wave] + 0.1, lambda wave=wave: student_rows(wave))

    s_yg = [new_send() for _ in range(3)]
    r_yg = {(d, k, a): new_recv() for d in "RL" for k in range(4) for a in range(3)}

    def term(k, a):
        owner = lax.rem(yo + k, 8)
        rel = lax.rem(owner // 2 - xo + 4, 4)
        cols = pl.ds(pl.multiple_of(lax.rem(owner, 2) * 512, 512), 512)
        if a == 0:
            grad[k, 0:256, :] = jnp.dot(
                gt[0:256, :], act[rel, :, cols], preferred_element_type=F32
            ).astype(BF16)
        else:
            grad[k, 256:384, :] = jnp.dot(
                gt[256:384, :], dout[rel, :, cols], preferred_element_type=F32
            ).astype(BF16)

    def yg_ref(d, k, a):
        if k == 0:
            return ring.at[0 if d == "R" else 1, 0, a, pl.ds(0 if d == "R" else 64, 64)]
        return ring.at[0 if d == "R" else 1, k, a]

    def yg_send(d, k, a):
        if k == 0:
            src = grad.at[4, pl.ds(a * 128 + (0 if d == "R" else 64), 64)]
        else:
            src = grad.at[4 - k if d == "R" else 4 + k, pl.ds(a * 128, 128)]
        send(src, yg_ref(d, k, a), s_yg[a], r_yg[d, k, a], y_dev(1 if d == "R" else -1))

    t_g = t_act[1] + 1.0

    def first_terms():
        term(4, 0)
        for a in range(2):
            for d in "RL":
                yg_send(d, 0, a)
        term(4, 1)
        for d in "RL":
            yg_send(d, 0, 2)
        for k in (3, 5):
            for a in range(2):
                term(k, a)

    agenda.at(t_g, first_terms)
    for i, k in enumerate((2, 6, 1, 7, 0)):
        for a in range(2):
            agenda.at(t_g + 8.0 + 3.2 * i + 1.5 * a, lambda k=k, a=a: term(k, a))

    def yg_hop(k, a):
        for d in "RL":
            wait_recv(yg_ref(d, k - 1, a), r_yg[d, k - 1, a])
            way = 0 if d == "R" else 1
            mine = 4 - k if d == "R" else 4 + k
            lo, n = a * 128, 128
            off = 0
            if k == 1:
                off, n = (0, 64) if d == "R" else (64, 64)
            grad[mine, lo + off : lo + off + n, :] = (
                grad[mine, lo + off : lo + off + n, :].astype(F32)
                + ring[way, k - 1, a, off : off + n, :].astype(F32)
            ).astype(BF16)
            yg_send(d, k, a)

    for k in range(1, 4):
        for a in range(3):
            agenda.at(t_g + 3.0 + 8.9 * (k - 1) + 2.95 * a, lambda k=k, a=a: yg_hop(k, a))

    def yg_last(a):
        for d in "RL":
            wait_recv(yg_ref(d, 3, a), r_yg[d, 3, a])
        total = (
            grad[0, a * 128 : a * 128 + 128, :].astype(F32)
            + ring[0, 3, a].astype(F32)
            + ring[1, 3, a].astype(F32)
        )
        if a == 0:
            gg_out[...] = total.T
            store(1, gg_out, gg_hbm)
        elif a == 1:
            gu_out[...] = total.T
            store(2, gu_out, gu_hbm)
        else:
            gd_out[...] = total
            store(3, gd_out, gd_hbm)

    for a in range(3):
        agenda.at(t_g + 3.0 + 8.9 * 3 + 2.95 * a, lambda a=a: yg_last(a))
        drain(grad.at[pl.ds(1, 7), pl.ds(a * 128, 128)], s_yg[a])

    agenda.run()
    for step in drains:
        step()
    for copy in stores:
        copy.wait()


def hand_over(*refs):
    for src, dst in zip(refs[:4], refs[4:]):
        dst[...] = src[...]


def body(*args):
    any_spec = pl.BlockSpec(memory_space=pl.ANY)
    vmem = pl.BlockSpec(memory_space=pltpu.VMEM)
    scratch = [
        pltpu.VMEM((4, 512, 1024), BF16),
        pltpu.VMEM((4, 512, 1024), BF16),
        pltpu.VMEM((4, 512, 1024), BF16),
        pltpu.VMEM((4096, 256), BF16),
        pltpu.VMEM((512, 1024), BF16),
        pltpu.VMEM((4096, 256), BF16),
        pltpu.VMEM((8, 128, 512), BF16),
        pltpu.VMEM((512, 512), BF16),
        pltpu.VMEM((2, 8, 16, 128), BF16),
        pltpu.VMEM((512, 1024), BF16),
        pltpu.VMEM((512, 1024), BF16),
        pltpu.VMEM((8, 32, 1024), BF16),
        pltpu.VMEM((512, 256), F32),
        pltpu.VMEM((512, 128), F32),
        pltpu.VMEM((384, 512), BF16),
        pltpu.VMEM((8, 384, 512), BF16),
        pltpu.VMEM((2, 4, 3, 128, 512), BF16),
        pltpu.VMEM((32, 1024), BF16),
        pltpu.VMEM((512, 128), F32),
        pltpu.VMEM((512, 128), F32),
        pltpu.VMEM((128, 512), F32),
        pltpu.SemaphoreType.DMA((N_SEND,)),
        pltpu.SemaphoreType.DMA((N_RECV,)),
        pltpu.SemaphoreType.DMA((12,)),
    ]
    shapes = (
        jax.ShapeDtypeStruct((32, 1024), BF16),
        jax.ShapeDtypeStruct((512, 128), F32),
        jax.ShapeDtypeStruct((512, 128), F32),
        jax.ShapeDtypeStruct((128, 512), F32),
    )
    results = pl.pallas_call(
        kernel,
        out_shape=shapes,
        in_specs=[any_spec, vmem, vmem] + [any_spec] * 7,
        out_specs=(any_spec,) * 4,
        scratch_shapes=scratch,
        compiler_params=pltpu.CompilerParams(
            collective_id=1, has_side_effects=True, vmem_limit_bytes=62 * 1024 * 1024
        ),
        cost_estimate=pl.CostEstimate(flops=5_000_000_000, bytes_accessed=12_000_000, transcendentals=400_000),
        name="distill_window",
    )(args[0], args[1].T, args[2].T, *args[3:])
    return pl.pallas_call(
        hand_over,
        out_shape=shapes,
        in_specs=[vmem] * 4,
        out_specs=(vmem,) * 4,
        compiler_params=pltpu.CompilerParams(vmem_limit_bytes=62 * 1024 * 1024),
        cost_estimate=pl.CostEstimate(flops=0, bytes_accessed=1_700_000, transcendentals=0),
        name="hand_over",
    )(*results)


def solution(mesh):
    in_specs = (
        P(("seq", "exp"), "tp"),
        P(("seq", "exp"), None),
        P(("seq", "exp"), None),
        P("exp", None, "tp"),
        P("exp", None, "tp"),
        P("exp", None, "tp"),
        P("seq", ("exp", "tp")),
        P("seq", ("exp", "tp")),
        P(("exp", "tp"), "seq"),
        P(("seq", "exp"), "tp"),
    )
    out_specs = (
        P(("seq", "exp"), "tp"),
        P("seq", ("exp", "tp")),
        P("seq", ("exp", "tp")),
        P(("exp", "tp"), "seq"),
    )
    return jax.shard_map(body, mesh=mesh, in_specs=in_specs, out_specs=out_specs, check_vma=False)
```

time: 138 us -> 124 us (0.90)
  local copies, waits for them, and re-layouts: 7.98 us -> 0 us
  Pallas kernels: 129 us -> 123 us
    unnamed x18 -> x0, local copies, waits for them, and re-layouts: 7.98 us -> none
    pallas_call x1 -> x2, Pallas kernels: 129 us -> 123 us  [the longest x1 121 us: body(): pl.pallas_call(kernel, out_shape=shapes, in_specs=[any_spec, vmem, vmem]...]
where the time goes in v2:
time: 124 us
  Pallas kernels  123 us (99%)
    pallas_call x1, Pallas kernels, body(): pl.pallas_call(kernel, out_shape=shapes, in_specs=[any_spec, vmem, vmem]...  121 us

profile of v2, /device:TPU:1, one launch (start us, length us, event | category | flops | bytes accessed | tf_op | source)
XLA Modules:
  0.0 123.5 jit_solution(8119863731652832221)
XLA Ops:
  0.6 120.8 %distill_window.1 = (bf16[32,1024]{1,0:T(8,128)(2,1)}, f32[512,128]{1,0:T(8,128)}, f32[512,128]{1,0:T(8,128)}, f32[128,512]{1,0:T(8,128)}) custom-call(bf16[32,1024]{1,0:T(8,128)(2,1)} %tokens.1, s32[8,32]{1,0:T(8,128)} %bitcast.2, f32[8,32]{1,0:T(8,128)} %bitcast.3, bf16[1,4096,128]{2,1,0:T(8,128)(2,1)} %egate.1, bf16[1,4096,128]{2,1,0:T(8,128)(2,1)} %eup.1, ...), custom_call_target="tpu_custom_call" | custom-call | flops 5000000000 | bytes 12000000 | tf_op jit(solution)/shard_map/distill_window/pallas_call | solution.py:662
  121.4 2.1 %hand_over.1 = (bf16[32,1024]{1,0:T(8,128)(2,1)}, f32[512,128]{1,0:T(8,128)}, f32[512,128]{1,0:T(8,128)}, f32[128,512]{1,0:T(8,128)}) custom-call(bf16[32,1024]{1,0:T(8,128)(2,1)} %get-tuple-element.8.refs_0_, f32[512,128]{1,0:T(8,128)} %get-tuple-element.9.refs_1_, f32[512,128]{1,0:T(8,128)} %get-tuple-element.10.refs_2_, f32[128,512]{1,0:T(8,128)} %get-tuple-element.11.refs_3_), custom_call_target="tpu_custom_call" | custom-call | bytes 1700000 | tf_op jit(solution)/shard_map/hand_over/pallas_call | solution.py:674

commit v3 on v2

--- a/solution.py
+++ b/solution.py
@@ -176,8 +176,9 @@
         def z0_ref(z, d, k):
             return buf.at[0, pl.ds(row_of(z), 32), part_cols[d] if k == 4 else cols0]
 
-        def z0_send(d, k):
-            send(z0_ref(came(d, k - 1), d, k), z0_ref(came(d, k), d, k), s_z0, r_z0[d, k], step_dev[d])
+        def z0_send(d, k, reach):
+            device = z_dev(reach if d == "R" else -reach)
+            send(z0_ref(came(d, k - reach), d, k), z0_ref(came(d, k), d, k), s_z0, r_z0[d, k], device)
 
         def piece_ref(rel, k, cols=cols0, other=0):
             pos, n = pieces[k]
@@ -205,26 +206,27 @@
                 s_b1, r_b1[0 if Z_POS[z] < 5 else 1], sib,
             )
 
-        plan = {("begin",): 0.0, ("ready", 0): 13.5, ("ready", 1): 16.6}
-        for k, (there, beyond) in enumerate(((3.1, 11.0), (6.8, 11.5), (9.8, 12.3), (12.7, 15.4), (14.6, 15.5))):
-            plan["x0", k] = 2.9 * k + 0.01
-            plan["x0_done", k], plan["f0_done", k] = there, beyond
-        plan["x1",] = 2.95
-        for k in range(1, 5):
-            plan["z0", k] = 2.9 * k
-            for c, when in ((0, 0.2), (1, 2.5), (3, 3.0), (2, 3.5)):
-                plan["z1", k, c] = 2.9 * k + when
+        plan = {("begin",): 0.0, ("x1",): 2.95, ("ready", 0): 12.24, ("ready", 1): 16.6}
+        for k, (here, start, there, beyond) in enumerate(
+            ((0, 0.01, 3.3, 11.6), (2.9, 2.91, 6.5, 11.6), (4.2, 4.21, 8.35, 12.0), (8.4, 8.41, 11.4, 15.3), (9.45, 9.46, 12.15, 15.35))
+        ):
+            plan["x0", k], plan["x0_done", k], plan["f0_done", k] = start, there, beyond
+            if k:
+                plan["z0", k] = here
+                for c, when in ((0, 0.2 if k < 2 else 0.65), (1, 2.5), (3, 3.0), (2, 3.5)):
+                    plan["z1", k, c] = 2.9 * k + when
         plan.update(times or {})
 
         def at(name, step):
             agenda.at(t0 + plan[name], step)
 
         def begin():
-            for d in "RL":
-                z0_send(d, 1)
             for d in (1, -1, 2):
                 send(z1_ref(0, 0), z1_ref(0, (-d) % 4), s_x1, r_x1[(-d) % 4], x_dev(d))
             for d in "RL":
+                z0_send(d, 1, 1)
+                z0_send(d, 2, 2)
+            for d in "RL":
                 z1_send(d, 1, 0)
 
         at(("begin",), begin)
@@ -232,8 +234,9 @@
         def z0_hop(k):
             for d in "RL":
                 wait_recv(z0_ref(came(d, k), d, k), r_z0[d, k])
-                if k < 4:
-                    z0_send(d, k + 1)
+                if k == 2:
+                    z0_send(d, 3, 1)
+                    z0_send(d, 4, 2)
 
         def x0_start(k):
             x0_piece(k)
@@ -343,10 +346,10 @@
                 yw_send(d, k + 1, a)
 
     agenda.at(0.01, yw_start)
+    yw_times = ((5.6, 6.1, 8.6), (11.4, 12.35, 13.46), (16.62, 20.35, 22.35), (23.05, 25.41, 26.05))
     for k in range(1, 5):
         for a in range(3):
-            when = 8.9 * (k - 1) + 2.95 * (a + 1) + 2.0 if k < 4 else 8.9 * 3 + 1.5 * (a + 1) + 2.0
-            agenda.at(1.25 * when + 2.0, lambda k=k, a=a: yw_hop(k, a))
+            agenda.at(yw_times[k - 1][a], lambda k=k, a=a: yw_hop(k, a))
     drain(wgu.at[pl.ds(0, 3584), pl.ds(0, 128)], s_yw[0])
     drain(wgu.at[pl.ds(0, 3584), pl.ds(128, 128)], s_yw[1])
     drain(wd.at[pl.ds(0, 7)], s_yw[2])
@@ -370,15 +373,15 @@
     drain(coef.at[0], s_cb)
 
     t_tok = gather(tok, 0.0)
-    late = {("begin",): 11.0, ("x1",): 15.1, ("ready", 0): 31.0, ("ready", 1): 32.0}
+    late = {("begin",): 12.22, ("x1",): 16.65, ("ready", 0): 35.2, ("ready", 1): 35.21}
     for k, (when, start, there, beyond) in enumerate(
-        ((0, 18.3, 22.5, 27.0), (15.2, 18.4, 24.2, 28.0), (18.2, 20.7, 25.9, 29.0), (20.6, 22.6, 26.5, 30.0), (26.0, 26.1, 30.0, 30.1))
+        ((0, 16.68, 22.98, 35.13), (16.66, 20.3, 25.45, 35.13), (16.67, 22.96, 26.6, 35.13), (22.36, 22.97, 26.7, 35.13), (22.37, 22.98, 26.8, 35.13))
     ):
         late["x0", k], late["x0_done", k], late["f0_done", k] = start, there, beyond
         if k:
             late["z0", k] = when
             for c in range(4):
-                late["z1", k, c] = when + (0.1 if k < 3 else 2.0 if k == 3 else 0.4)
+                late["z1", k, c] = (20.5, 25.4, 26.5, 35.12)[k - 1]
     gather(dout, 0.0, late)
 
     def weight_wait():
@@ -429,7 +432,9 @@
     s_sp = [new_send() for _ in range(2)]
     r_sp = [new_recv() for _ in range(2)]
     s_rs = new_send()
-    r_rs = {z: new_recv() for z in range(1, 8)}
+    r_rs = {z: new_recv() for z in (1, 7)}
+    r_rs.update({(z, turn): new_recv() for z in (2, 3, 5, 6) for turn in range(2)})
+    r_rs4 = [new_recv() for _ in range(2)]
 
     def coef_column(other, wave):
         start, n = ((0, 5), (5, 3))[wave]
@@ -463,8 +468,23 @@
         if other == 1:
             send(part.at[rows], sibp.at[own], s_sp[wave], r_sp[wave], sib)
         else:
-            for z in ((2, 6, 1, 7), (4, 3, 5))[wave]:
-                send(part.at[pl.ds(row_of(z), 32)], rsb.at[8 - z], s_rs, r_rs[8 - z], z_dev(z))
+            if wave == 0:
+                for z in (1, 7):
+                    send(part.at[pl.ds(row_of(z), 32)], rsb.at[8 - z], s_rs, r_rs[8 - z], z_dev(z))
+            else:
+                for turn in range(2):
+                    for z, step, i in ((3, 1, 0), (5, -1, 1)):
+                        half = pl.ds(512 * (i ^ 1 ^ turn), 512)
+                        send(
+                            part.at[pl.ds(row_of(z), 32), half], rsb.at[8 - z, :, half],
+                            s_rs, r_rs[8 - z, turn], z_dev(step),
+                        )
+                        if turn == 0:
+                            half = pl.ds(512 * i, 512)
+                            send(
+                                part.at[pl.ds(row_of(4), 32), half], rsb.at[4, :, half],
+                                s_rs, r_rs4[i], z_dev(2 * step),
+                            )
 
     t_down = [20.2, 22.9]
     for wave in range(2):
@@ -478,11 +498,31 @@
         drain(part.at[pl.ds(first + n, n)], s_sp[wave])
     drain(part.at[pl.ds(0, 224)], s_rs)
 
+    def teacher_relay(turn):
+        for i, (z, far) in enumerate(((2, 5), (6, 3))):
+            start = 512 * (i ^ 1 ^ turn)
+            half = pl.ds(start, 512)
+            rows = pl.ds(row_of(z), 32)
+            wait_recv(rsb.at[far, :, half], r_rs[far, turn])
+            total = part[rows, half].astype(F32) + rsb[far, :, half].astype(F32)
+            if turn == 1:
+                wait_recv(rsb.at[4, :, half], r_rs4[i])
+                total = total + rsb[4, :, half].astype(F32)
+            part[rows, half] = total.astype(BF16)
+            send(part.at[rows, half], rsb.at[8 - z, :, half], s_rs, r_rs[8 - z, turn], z_dev(z))
+
+    for turn in range(2):
+        agenda.at(26.0 + 0.1 * turn, lambda turn=turn: teacher_relay(turn))
+
     def teacher_sum():
         total = part[0:32, :].astype(F32)
-        for z in (1, 7, 2, 6, 3, 5, 4):
-            wait_recv(rsb.at[z], r_rs[z])
-        for z in range(1, 8):
+        for z in (1, 7, 2, 6):
+            if z in (1, 7):
+                wait_recv(rsb.at[z], r_rs[z])
+            else:
+                for turn in range(2):
+                    half = pl.ds(512 * ((0 if z == 6 else 1) ^ 1 ^ turn), 512)
+                    wait_recv(rsb.at[z, :, half], r_rs[z, turn])
             total = total + rsb[z].astype(F32)
         row = total.astype(BF16)
         t_out[...] = row
@@ -505,8 +545,8 @@
         hg[...] = total
 
     t_act = gather(act, t_sum + 0.1)
-    for rel, when in enumerate((1.0, 4.0, 7.0, 10.0)):
-        agenda.at(max(45.5, t_sum + 0.1 + when), lambda rel=rel: student_back(rel))
+    for rel, when in enumerate((0.2, 0.2, 4.3, 4.3)):
+        agenda.at(t_sum + 0.1 + when, lambda rel=rel: student_back(rel))
 
     def student_rows(wave):
         first, n = WAVES[wave]

time: 124 us -> 120 us (0.968)
  Pallas kernels: 123 us -> 119 us
    pallas_call x1, Pallas kernels: 121 us -> 117 us  [body(): pl.pallas_call(kernel, out_shape=shapes, in_specs=[any_spec, vmem, vmem]...]
where the time goes in v3:
time: 120 us; the launch traced here: 119 us
  Pallas kernels  119 us (99%)
    pallas_call x1, Pallas kernels, body(): pl.pallas_call(kernel, out_shape=shapes, in_specs=[any_spec, vmem, vmem]...  117 us

profile of v3, /device:TPU:1, one launch (start us, length us, event | category | flops | bytes accessed | tf_op | source)
XLA Modules:
  0.0 119.4 jit_solution(14578670908345934327)
XLA Ops:
  0.6 116.7 %distill_window.1 = (bf16[32,1024]{1,0:T(8,128)(2,1)}, f32[512,128]{1,0:T(8,128)}, f32[512,128]{1,0:T(8,128)}, f32[128,512]{1,0:T(8,128)}) custom-call(bf16[32,1024]{1,0:T(8,128)(2,1)} %tokens.1, s32[8,32]{1,0:T(8,128)} %bitcast.2, f32[8,32]{1,0:T(8,128)} %bitcast.3, bf16[1,4096,128]{2,1,0:T(8,128)(2,1)} %egate.1, bf16[1,4096,128]{2,1,0:T(8,128)(2,1)} %eup.1, ...), custom_call_target="tpu_custom_call" | custom-call | flops 5000000000 | bytes 12000000 | tf_op jit(solution)/shard_map/distill_window/pallas_call | solution.py:702
  117.3 2.1 %hand_over.1 = (bf16[32,1024]{1,0:T(8,128)(2,1)}, f32[512,128]{1,0:T(8,128)}, f32[512,128]{1,0:T(8,128)}, f32[128,512]{1,0:T(8,128)}) custom-call(bf16[32,1024]{1,0:T(8,128)(2,1)} %get-tuple-element.8.refs_0_, f32[512,128]{1,0:T(8,128)} %get-tuple-element.9.refs_1_, f32[512,128]{1,0:T(8,128)} %get-tuple-element.10.refs_2_, f32[128,512]{1,0:T(8,128)} %get-tuple-element.11.refs_3_), custom_call_target="tpu_custom_call" | custom-call | bytes 1700000 | tf_op jit(solution)/shard_map/hand_over/pallas_call | solution.py:714

commit v4 on v3

--- a/solution.py
+++ b/solution.py
@@ -10,8 +10,8 @@
 BF16 = jnp.bfloat16
 Z_ORDER = (0, 1, 7, 2, 6, 3, 5, 4)
 Z_POS = {z: i for i, z in enumerate(Z_ORDER)}
-N_RECV = 400
-N_SEND = 96
+N_RECV = 280
+N_SEND = 40
 
 
 WAVES = ((0, 160), (320, 96))
@@ -45,7 +45,7 @@
 def kernel(
     tokens, ids, weights, egate, eup, edown, sgate, sup, sdown, ograd,
     t_hbm, gg_hbm, gu_hbm, gd_hbm,
-    tok, act, dout, wt, wed, wgu, wd, hid, coef, part, sibp, rsb, gu, hg, gt, grad, ring, t_out, gg_out, gu_out, gd_out,
+    tok, act, dout, wt, wed, wgu, wd, hid, coef, part, sibp, rsb, gu, hg, gt, grad, ring, t_out, gg_out, gu_out, gd_out, ids_v, weights_v,
     send_sems, recv_sems, local_sems,
 ):
     yo = lax.axis_index("seq")
@@ -99,6 +99,11 @@
 
         drains.append(step)
 
+    barrier = pltpu.get_barrier_semaphore()
+    peers = [z_dev(d) for d in range(1, 8)] + [x_dev(d) for d in range(1, 4)] + [y_dev(1), y_dev(-1), sib]
+    for device in peers:
+        pl.semaphore_signal(barrier, inc=1, device_id=device, device_id_type=MESH)
+
     local = []
 
     def load(src, dst):
@@ -114,10 +119,11 @@
         load(sdown, wd.at[yo]),
         load(ograd, dout.at[0, pl.ds(0, 32)]),
     ]
+    routes = [load(ids, ids_v), load(weights, weights_v)]
     stores = []
 
     def store(i, src, dst):
-        copy = pltpu.make_async_copy(src, dst, local_sems.at[8 + i])
+        copy = pltpu.make_async_copy(src, dst, local_sems.at[10 + i])
         copy.start()
         stores.append(copy)
 
@@ -126,30 +132,6 @@
         load(eup.at[0], wt.at[:, pl.ds(128, 128)]),
         load(edown.at[0], wed),
     ]
-
-    barrier = pltpu.get_barrier_semaphore()
-    peers = [z_dev(d) for d in range(1, 8)] + [x_dev(d) for d in range(1, 4)] + [y_dev(1), y_dev(-1), sib]
-    for device in peers:
-        pl.semaphore_signal(barrier, inc=1, device_id=device, device_id_type=MESH)
-
-    lane = lax.broadcasted_iota(jnp.int32, (16, 128), 1)
-    lane_e = lax.rem(lane, 16)
-    lane_half = lax.rem(lane // 16, 2)
-    blank = jnp.zeros((8, 96), jnp.int32)
-    names = jnp.concatenate([ids[...], blank], axis=1).T
-    shares = jnp.concatenate([weights[...], blank.astype(F32)], axis=1).T
-    halves = []
-    for half in range(2):
-        total = jnp.zeros((16, 128), F32)
-        for k in range(8):
-            name = names[half * 16 : half * 16 + 16, k : k + 1]
-            weight = shares[half * 16 : half * 16 + 16, k : k + 1]
-            total = total + jnp.where(lane_e == name, weight, 0.0)
-        halves.append(total)
-    value = jnp.where(lane_half == 0, halves[0], halves[1])
-    high = value.astype(BF16).astype(F32)
-    value = jnp.where(lane < 32, high, jnp.where(lane < 64, value - high, 0.0))
-    coef[0, 0] = value.astype(BF16)
 
     pl.semaphore_wait(barrier, len(peers))
     for copy in first:
@@ -346,7 +328,7 @@
                 yw_send(d, k + 1, a)
 
     agenda.at(0.01, yw_start)
-    yw_times = ((5.6, 6.1, 8.6), (11.4, 12.35, 13.46), (16.62, 20.35, 22.35), (23.05, 25.41, 26.05))
+    yw_times = ((5.6, 6.1, 8.6), (11.4, 12.35, 13.46), (16.62, 20.35, 23.11), (25.46, 26.05, 26.65))
     for k in range(1, 5):
         for a in range(3):
             agenda.at(yw_times[k - 1][a], lambda k=k, a=a: yw_hop(k, a))
@@ -359,6 +341,26 @@
     r_cb = new_recv()
 
     def coef_start():
+        for copy in routes:
+            copy.wait()
+        lane = lax.broadcasted_iota(jnp.int32, (16, 128), 1)
+        lane_e = lax.rem(lane, 16)
+        lane_half = lax.rem(lane // 16, 2)
+        blank = jnp.zeros((8, 96), jnp.int32)
+        names = jnp.concatenate([ids_v[...], blank], axis=1).T
+        shares = jnp.concatenate([weights_v[...], blank.astype(F32)], axis=1).T
+        halves = []
+        for half in range(2):
+            total = jnp.zeros((16, 128), F32)
+            for k in range(8):
+                name = names[half * 16 : half * 16 + 16, k : k + 1]
+                weight = shares[half * 16 : half * 16 + 16, k : k + 1]
+                total = total + jnp.where(lane_e == name, weight, 0.0)
+            halves.append(total)
+        value = jnp.where(lane_half == 0, halves[0], halves[1])
+        high = value.astype(BF16).astype(F32)
+        value = jnp.where(lane < 32, high, jnp.where(lane < 64, value - high, 0.0))
+        coef[0, 0] = value.astype(BF16)
         for z in range(1, 8):
             send(coef.at[0, 0], coef.at[0, Z_POS[8 - z]], s_co, r_co[8 - z], z_dev(z))
 
@@ -373,15 +375,15 @@
     drain(coef.at[0], s_cb)
 
     t_tok = gather(tok, 0.0)
-    late = {("begin",): 12.22, ("x1",): 16.65, ("ready", 0): 35.2, ("ready", 1): 35.21}
+    late = {("begin",): 12.22, ("x1",): 16.55, ("ready", 0): 35.2, ("ready", 1): 35.21}
     for k, (when, start, there, beyond) in enumerate(
-        ((0, 16.68, 22.98, 35.13), (16.66, 20.3, 25.45, 35.13), (16.67, 22.96, 26.6, 35.13), (22.36, 22.97, 26.7, 35.13), (22.37, 22.98, 26.8, 35.13))
+        ((0, 16.69, 23.12, 35.13), (16.56, 20.3, 25.45, 35.13), (16.68, 22.96, 26.6, 35.13), (25.41, 25.42, 26.7, 35.13), (25.41, 25.43, 26.8, 35.13))
     ):
         late["x0", k], late["x0_done", k], late["f0_done", k] = start, there, beyond
         if k:
             late["z0", k] = when
             for c in range(4):
-                late["z1", k, c] = (20.5, 25.4, 26.5, 35.12)[k - 1]
+                late["z1", k, c] = (20.5, 23.1, 26.5, 35.12)[k - 1]
     gather(dout, 0.0, late)
 
     def weight_wait():
@@ -390,7 +392,7 @@
 
     agenda.at(t_tok[0] + 0.01, weight_wait)
     s_hid = [new_send() for _ in range(2)]
-    r_hid = {(d, w): new_recv() for d in (1, 2, 3) for w in range(2)}
+    r_hid = {(d, w, other): new_recv() for d in (1, 2, 3) for w in range(2) for other in range(2)}
 
     def hid_cols(d):
         return pl.ds(pl.multiple_of(lax.rem(xo + d, 4) * 128, 128), 128)
@@ -421,9 +423,11 @@
         gate = gu[rows, 0:128]
         up = gu[rows, 128:256]
         hid[rows, hid_cols(0)] = (gate * sigmoid(gate) * up).astype(BF16)
-        ref = hid.at[rows, hid_cols(0)]
-        for d in (1, 3, 2):
-            send(ref, ref, s_hid[wave], r_hid[4 - d, wave], x_dev(d))
+        first, n = WAVES[wave]
+        for other in (1, 0):
+            ref = hid.at[pl.ds(first + other * n, n), hid_cols(0)]
+            for d in (1, 3, 2):
+                send(ref, ref, s_hid[wave], r_hid[4 - d, wave, other], x_dev(d))
 
     for wave in range(2):
         agenda.at(t_tok[wave] + 0.02, lambda wave=wave: teacher_hidden(wave))
@@ -447,8 +451,6 @@
         return jnp.concatenate(cols, axis=1).reshape(n * 32, 1)
 
     def hid_wait(wave):
-        for d in (1, 3, 2):
-            wait_recv(hid.at[wave_rows(wave), hid_cols(d)], r_hid[d, wave])
         if wave == 0:
             wait_recv(coef.at[1], r_cb)
 
@@ -457,6 +459,8 @@
         rows = pl.ds(first + other * n, n)
         own = pl.ds(first, n)
         scale = coef_column(other, wave)
+        for d in (1, 3, 2):
+            wait_recv(hid.at[rows, hid_cols(d)], r_hid[d, wave, other])
         if other == 0:
             wait_recv(sibp.at[own], r_sp[wave])
         for q in range(2):
@@ -545,7 +549,7 @@
         hg[...] = total
 
     t_act = gather(act, t_sum + 0.1)
-    for rel, when in enumerate((0.2, 0.2, 4.3, 4.3)):
+    for rel, when in enumerate((0.2, 0.2, 6.55, 6.55)):
         agenda.at(t_sum + 0.1 + when, lambda rel=rel: student_back(rel))
 
     def student_rows(wave):
@@ -689,9 +693,11 @@
         pltpu.VMEM((512, 128), F32),
         pltpu.VMEM((512, 128), F32),
         pltpu.VMEM((128, 512), F32),
+        pltpu.VMEM((8, 32), jnp.int32),
+        pltpu.VMEM((8, 32), F32),
         pltpu.SemaphoreType.DMA((N_SEND,)),
         pltpu.SemaphoreType.DMA((N_RECV,)),
-        pltpu.SemaphoreType.DMA((12,)),
+        pltpu.SemaphoreType.DMA((14,)),
     ]
     shapes = (
         jax.ShapeDtypeStruct((32, 1024), BF16),
@@ -702,7 +708,7 @@
     results = pl.pallas_call(
         kernel,
         out_shape=shapes,
-        in_specs=[any_spec, vmem, vmem] + [any_spec] * 7,
+        in_specs=[any_spec] * 10,
         out_specs=(any_spec,) * 4,
         scratch_shapes=scratch,
         compiler_params=pltpu.CompilerParams(

time: 120 us -> 116 us (0.967)
  Pallas kernels: 119 us -> 116 us
    pallas_call x1, Pallas kernels: 117 us -> 114 us  [body(): pl.pallas_call(kernel, out_shape=shapes, in_specs=[any_spec] * 10, out_sp...]
where the time goes in v4:
time: 116 us
  Pallas kernels  116 us (100%)
    pallas_call x1, Pallas kernels, body(): pl.pallas_call(kernel, out_shape=shapes, in_specs=[any_spec] * 10, out_sp...  114 us

profile of v4, /device:TPU:1, one launch (start us, length us, event | category | flops | bytes accessed | tf_op | source)
XLA Modules:
  0.0 116.3 jit_solution(12953924196394107837)
XLA Ops:
  0.6 113.6 %distill_window.1 = (bf16[32,1024]{1,0:T(8,128)(2,1)}, f32[512,128]{1,0:T(8,128)}, f32[512,128]{1,0:T(8,128)}, f32[128,512]{1,0:T(8,128)}) custom-call(bf16[32,1024]{1,0:T(8,128)(2,1)} %tokens.1, s32[8,32]{1,0:T(8,128)} %bitcast.2, f32[8,32]{1,0:T(8,128)} %bitcast.3, bf16[1,4096,128]{2,1,0:T(8,128)(2,1)} %egate.1, bf16[1,4096,128]{2,1,0:T(8,128)(2,1)} %eup.1, ...), custom_call_target="tpu_custom_call" | custom-call | flops 5000000000 | bytes 12000000 | tf_op jit(solution)/shard_map/distill_window/pallas_call | solution.py:708
  114.2 2.1 %hand_over.1 = (bf16[32,1024]{1,0:T(8,128)(2,1)}, f32[512,128]{1,0:T(8,128)}, f32[512,128]{1,0:T(8,128)}, f32[128,512]{1,0:T(8,128)}) custom-call(bf16[32,1024]{1,0:T(8,128)(2,1)} %get-tuple-element.8.refs_0_, f32[512,128]{1,0:T(8,128)} %get-tuple-element.9.refs_1_, f32[512,128]{1,0:T(8,128)} %get-tuple-element.10.refs_2_, f32[128,512]{1,0:T(8,128)} %get-tuple-element.11.refs_3_), custom_call_target="tpu_custom_call" | custom-call | bytes 1700000 | tf_op jit(solution)/shard_map/hand_over/pallas_call | solution.py:720

commit v5 on v4

--- a/solution.py
+++ b/solution.py
@@ -112,7 +112,7 @@
         local.append(copy)
         return copy
 
-    first = [
+    blocks = [
         load(tokens, tok.at[0, pl.ds(0, 32)]),
         load(sgate, wgu.at[pl.ds(pl.multiple_of(yo * 512, 512), 512), pl.ds(0, 128)]),
         load(sup, wgu.at[pl.ds(pl.multiple_of(yo * 512, 512), 512), pl.ds(128, 128)]),
@@ -134,8 +134,7 @@
     ]
 
     pl.semaphore_wait(barrier, len(peers))
-    for copy in first:
-        copy.wait()
+    blocks[0].wait()
 
     def gather(buf, t0, times=None):
         s_z0, s_x0, s_f0, s_b0 = new_send(), [new_send() for _ in range(2)], new_send(), new_send()
@@ -148,7 +147,6 @@
         r_x1 = {rel: new_recv() for rel in (1, 2, 3)}
         r_z1 = {(d, k, c): new_recv() for d in "RL" for k in range(1, 5) for c in range(4)}
         r_b0, r_b1 = [new_recv() for _ in range(2)], [new_recv() for _ in range(2)]
-        step_dev = {"R": z_dev(1), "L": z_dev(-1)}
         cols0, cols1 = pl.ds(0, Z_FIRST), pl.ds(Z_FIRST, 1024 - Z_FIRST)
         part_cols = {"R": pl.ds(0, 384), "L": pl.ds(384, Z_FIRST - 384)}
 
@@ -175,8 +173,9 @@
         def z1_ref(z, c):
             return buf.at[c, pl.ds(row_of(z), 32), cols1]
 
-        def z1_send(d, k, c):
-            send(z1_ref(came(d, k - 1), c), z1_ref(came(d, k), c), s_z1, r_z1[d, k, c], step_dev[d])
+        def z1_send(d, k, c, reach=1):
+            device = z_dev(reach if d == "R" else -reach)
+            send(z1_ref(came(d, k - reach), c), z1_ref(came(d, k), c), s_z1, r_z1[d, k, c], device)
 
         def b0_send(rel, k):
             send(piece_ref(rel, k), piece_ref(rel, k, other=1), s_b0, r_b0[0 if k < 3 else 1], sib)
@@ -268,8 +267,10 @@
                     continue
                 z = came(d, k)
                 wait_recv(z1_ref(z, c), r_z1[d, k, c])
-                if k < 3 or (k == 3 and (d == "R") == (c in (0, 1))):
+                if k < 3:
                     z1_send(d, k + 1, c)
+                if k == (2 if times is None else 3) and (d == "R") == (c in (0, 1)):
+                    z1_send(d, 4, c, 4 - k)
                 if c == 2:
                     b1_send(z)
 
@@ -317,6 +318,8 @@
         send(ref, ref, s_yw[a], r_yw[d, k, a], y_dev(1 if d == "R" else -1))
 
     def yw_start():
+        for copy in blocks[1:]:
+            copy.wait()
         for a in range(3):
             for d in "RL":
                 yw_send(d, 1, a)
@@ -664,13 +667,20 @@
 
 
 def hand_over(*refs):
-    for src, dst in zip(refs[:4], refs[4:]):
-        dst[...] = src[...]
+    ins, outs, held, sems = refs[:4], refs[4:8], refs[8:12], refs[12]
+    loads = [pltpu.make_async_copy(ins[i], held[i], sems.at[i]) for i in range(4)]
+    writes = [pltpu.make_async_copy(held[i], outs[i], sems.at[4 + i]) for i in range(4)]
+    for load in loads:
+        load.start()
+    for load, write in zip(loads, writes):
+        load.wait()
+        write.start()
+    for write in writes:
+        write.wait()
 
 
 def body(*args):
     any_spec = pl.BlockSpec(memory_space=pl.ANY)
-    vmem = pl.BlockSpec(memory_space=pltpu.VMEM)
     scratch = [
         pltpu.VMEM((4, 512, 1024), BF16),
         pltpu.VMEM((4, 512, 1024), BF16),
@@ -720,8 +730,9 @@
     return pl.pallas_call(
         hand_over,
         out_shape=shapes,
-        in_specs=[vmem] * 4,
-        out_specs=(vmem,) * 4,
+        in_specs=[any_spec] * 4,
+        out_specs=(any_spec,) * 4,
+        scratch_shapes=[pltpu.VMEM(shape.shape, shape.dtype) for shape in shapes] + [pltpu.SemaphoreType.DMA((8,))],
         compiler_params=pltpu.CompilerParams(vmem_limit_bytes=62 * 1024 * 1024),
         cost_estimate=pl.CostEstimate(flops=0, bytes_accessed=1_700_000, transcendentals=0),
         name="hand_over",

time: 116 us -> 116 us (level)
  no operation moved by 1% of the time
where the time goes in v5:
time: 116 us; the launch traced here: 115 us
  Pallas kernels  115 us (99%)
    pallas_call x1, Pallas kernels, body(): pl.pallas_call(kernel, out_shape=shapes, in_specs=[any_spec] * 10, out_sp...  113 us

profile of v5, /device:TPU:1, one launch (start us, length us, event | category | flops | bytes accessed | tf_op | source)
XLA Modules:
  0.0 115.5 jit_solution(12997362397346036560)
XLA Ops:
  0.6 112.9 %distill_window.1 = (bf16[32,1024]{1,0:T(8,128)(2,1)}, f32[512,128]{1,0:T(8,128)}, f32[512,128]{1,0:T(8,128)}, f32[128,512]{1,0:T(8,128)}) custom-call(bf16[32,1024]{1,0:T(8,128)(2,1)} %tokens.1, s32[8,32]{1,0:T(8,128)} %bitcast.2, f32[8,32]{1,0:T(8,128)} %bitcast.3, bf16[1,4096,128]{2,1,0:T(8,128)(2,1)} %egate.1, bf16[1,4096,128]{2,1,0:T(8,128)(2,1)} %eup.1, ...), custom_call_target="tpu_custom_call" | custom-call | flops 5000000000 | bytes 12000000 | tf_op jit(solution)/shard_map/distill_window/pallas_call | solution.py:718
  113.5 1.9 %hand_over.1 = (bf16[32,1024]{1,0:T(8,128)(2,1)}, f32[512,128]{1,0:T(8,128)}, f32[512,128]{1,0:T(8,128)}, f32[128,512]{1,0:T(8,128)}) custom-call(bf16[32,1024]{1,0:T(8,128)(2,1)} %get-tuple-element.8.refs_0_, f32[512,128]{1,0:T(8,128)} %get-tuple-element.9.refs_1_, f32[512,128]{1,0:T(8,128)} %get-tuple-element.10.refs_2_, f32[128,512]{1,0:T(8,128)} %get-tuple-element.11.refs_3_), custom_call_target="tpu_custom_call" | custom-call | bytes 1700000 | tf_op jit(solution)/shard_map/hand_over/pallas_call | solution.py:730
